TPU v7x, 32 devices: a whole 2x2x4 slice. The times are simulated.
32 devices in a mesh: groups: 2 (over x), shard: 8 (over z, y), sub: 2 (over core).
Axes of the slice: x: 2, y: 2, z: 4, core: 2. Of those that a mesh axis runs over, the one named last changes fastest.
Arguments:
- queries: bfloat16 [256, 32, 128], P(('groups', 'shard', 'sub')), parts along dimension 0, may hold values from -1.796875 to 1.796875
- passages: bfloat16 [2048, 128, 128], P(('shard', 'sub')), may hold values from -1.796875 to 1.796875
- passage_len: int32 [2048], P(('shard', 'sub')), may hold values from 16 to 128, as said below
- slot_query: int32 [32, 16, 24], P('groups', ('shard', 'sub')), parts along dimension 0, may hold values from 0 to 7
- slot_passage: int32 [32, 16, 24], P('groups', ('shard', 'sub')), parts along dimension 0, may hold values from 0 to 127
- slot_count: int32 [32, 16], P('groups', ('shard', 'sub')), parts along dimension 0, may hold values from 1 to 24, as said below
Outputs:
- slot_score: float32 [32, 16, 24], P(('groups', 'shard', 'sub')), parts along dimension 0
There are 2 independent parts, one for each index of `groups`. A program takes and returns all parts, laid end to end along the dimension named above; an argument that names none is the same for every part. Nothing has to cross between parts.
Inputs may be any that keep to these rules, and one draw needn't show every extreme that they name: `passage_len`: live tokens of a passage; some passage has all 128. Live slots from one source to one owner are its first slot_count entries; some owner receives 24 live slots from every source.
All inputs are finite; a program needn't handle non-finite values.
Results may differ from a plain program's by a relative error of at most 0.0003.
Values may be sent and summed in bfloat16 or wider, within the bound.
No kernel may reach another device: no remote copies, remote signals or barrier semaphores. Data moves between devices by JAX's collectives and lax.ppermute only.
A program may use at most 64 MiB of HBM per device.

v0:
```python
import functools

import jax
import jax.numpy as jnp
from jax import lax
from jax.experimental import pallas as pl
from jax.experimental.pallas import tpu as pltpu
from jax.sharding import PartitionSpec as P

GROUPS = 8
CHUNKS = 8
SHIFT = 8
QUERY, PASSAGE, LENGTH, COUNT = 0, 32, 64, 96


def distance(call, i):
    return (jnp.where(i == 1, 1, i * 2), i + 2, i * 2 + 5)[call]


def list_groups(sizes, pack, per_source, row_ref, total_ref, work_refs):
    me = lax.axis_index("shard")
    for call, (n, work_ref) in enumerate(zip(sizes, work_refs)):

        def list_source(i, total):
            live = row_ref[jnp.bitwise_xor(me, distance(call, i)), COUNT]
            for g in range(per_source):
                work_ref[total + g] = (i << SHIFT) + g
            return total + lax.shift_right_logical(live + pack - 1, pack.bit_length() - 1)

        total = 0
        if n <= 8:
            for i in range(n):
                total = list_source(i, total)
        else:
            total = lax.fori_loop(0, n, list_source, 0)
        for g in range(GROUPS):
            work_ref[total + g] = 0
        total_ref[call] = total


def pack_kernel(shards, sizes, pack, per_source, *refs):
    query_hbm, passage_hbm, count_hbm, length_hbm, tokens_hbm, own_hbm, theirs_ref, tokens_ref, own_ref, add_ref = refs[:10]
    row_ref, total_ref, *work_refs = refs[10 : 12 + len(sizes)]
    mine_ref, query_ref, passage_ref, count_ref, length_ref, sems, own_sems, row_sem = refs[12 + len(sizes) :]
    copies = [
        pltpu.make_async_copy(src, dst, sems.at[i])
        for i, (src, dst) in enumerate(
            (
                (query_hbm, query_ref),
                (passage_hbm, passage_ref),
                (count_hbm, count_ref),
                (length_hbm, length_ref),
                (tokens_hbm, tokens_ref),
            )
        )
    ]
    size = own_ref.shape[0] // CHUNKS
    own_copies = [
        pltpu.make_async_copy(own_hbm.at[pl.ds(i * size, size)], own_ref.at[pl.ds(i * size, size)], own_sems.at[i])
        for i in range(CHUNKS)
    ]
    for copy in copies + own_copies:
        copy.start()
    row = lax.broadcasted_iota(jnp.int32, add_ref.shape, 0)
    col = lax.broadcasted_iota(jnp.int32, add_ref.shape, 1)
    q_bits = tokens_ref.shape[1].bit_length() - 1
    add_ref[...] = jnp.where(lax.shift_right_logical(row, q_bits) == col, 1.0, 0.0).astype(add_ref.dtype)
    for copy in copies:
        copy.wait()
    cap = query_ref.shape[1]
    lengths = length_ref[...].reshape(1, -1)
    counts = jnp.broadcast_to(count_ref[...].reshape(1, -1), (2 * shards, 2 * shards))
    row = lax.broadcasted_iota(jnp.int32, counts.shape, 0)
    col = lax.broadcasted_iota(jnp.int32, counts.shape, 1)
    counts = jnp.sum(jnp.where(row == col, counts, 0), axis=1, keepdims=True)
    blank = jnp.zeros((2 * shards, 32 - cap), jnp.int32)
    passage = jnp.concatenate([passage_ref[...], blank], axis=1)
    passage = jnp.concatenate([passage] * 4, axis=1)
    length = jnp.take_along_axis(jnp.broadcast_to(lengths, passage.shape), passage, axis=1)
    query = jnp.concatenate([jnp.concatenate([query_ref[...], blank], axis=1)] * 4, axis=1)
    lane = lax.broadcasted_iota(jnp.int32, passage.shape, 1)
    packed = jnp.where(lane < PASSAGE, query, jnp.where(lane < LENGTH, passage, jnp.where(lane < COUNT, length, counts)))
    packed = packed.reshape(shards, 2, 128)
    first = lax.axis_index("sub") == 0
    mine_ref[...] = jnp.where(first, packed[:, 0], packed[:, 1])
    theirs_ref[...] = jnp.where(first, packed[:, 1], packed[:, 0])
    copy = pltpu.make_async_copy(mine_ref, row_ref, row_sem)
    copy.start()
    copy.wait()
    list_groups(sizes, pack, per_source, row_ref, total_ref, work_refs)
    for copy in own_copies:
        copy.wait()


def score_kernel(shards, calls, call, pack, cap, *refs):
    distances = calls[call]
    n = len(distances)
    p = 1 if call == 1 else n
    lists, refs = [refs[:3]], refs[3:]
    if call == 0:
        other_rows, refs = refs[0], refs[1:]
        refs, (out_ref, *other_lists, query_ref, best_ref, row_sem) = refs[: p + 3], refs[p + 3 :]
        row_ref, total_ref, *work_refs = other_lists
        lists.append((row_ref, total_ref, work_refs[0]))
        copy = pltpu.make_async_copy(other_rows, row_ref, row_sem)
        copy.start()
    else:
        lists.append(refs[:3])
        refs, (out_ref, query_ref, best_ref) = refs[3:-3], refs[-3:]
    pieces, passage_refs, add_ref, earlier = refs[:p], refs[p : p + 2], refs[p + 2], refs[p + 3 :]
    q_tok, width = query_ref.shape[2:]
    tok_slots = passage_refs[0].shape[1]
    per_source = best_ref.shape[0]
    lanes = pack * q_tok
    q_bits = q_tok.bit_length() - 1
    me, core = lax.axis_index("shard"), lax.axis_index("sub")
    if call == 1:
        query_ref[...] = pieces[0][...]
    else:
        for i, piece in enumerate(reversed(pieces)):
            query_ref[i] = piece[...]
    best_ref[...] = jnp.zeros_like(best_ref)
    token = lax.broadcasted_iota(jnp.int32, (tok_slots, lanes), 0)
    place = lax.shift_right_logical(lax.broadcasted_iota(jnp.int32, (1, lanes), 1), q_bits)
    blank = jnp.zeros((q_tok, width), query_ref.dtype)

    for which, passages in enumerate(passage_refs):
        meta_ref, total_ref, work_ref = lists[which]
        owner = core if which == 0 else 1 - core
        if call == 0 and which == 1:
            copy.wait()
            list_groups(tuple(map(len, calls)), pack, per_source, row_ref, total_ref, work_refs)
        total = total_ref[call]

        def one_step(first_group, groups):
            for j in range(groups):
                work = work_ref[first_group + j]
                i, g = lax.shift_right_logical(work, SHIFT), jnp.bitwise_and(work, (1 << SHIFT) - 1)
                shard = jnp.bitwise_xor(me, distance(call, i))
                rows, cols, limit = [], [], jnp.zeros((1, lanes), jnp.int32)
                for a in range(pack):
                    slot = g * pack + a
                    query, passage = meta_ref[shard, QUERY + slot], meta_ref[shard, PASSAGE + slot]
                    rows.append(jnp.concatenate([blank] * a + [query_ref[i, query]] + [blank] * (pack - 1 - a), axis=1))
                    cols.append(passages[passage])
                    limit = jnp.where(place == a, meta_ref[shard, LENGTH + slot], limit)
                sims = lax.dot_general(
                    jnp.concatenate(cols, axis=1), jnp.concatenate(rows, axis=0),
                    (((1,), (1,)), ((), ())), preferred_element_type=jnp.float32,
                )
                best = jnp.max(jnp.where(token < limit, sims, -1e30), axis=0, keepdims=True)
                best = jnp.where(place + g * pack < meta_ref[shard, COUNT], best, 0.0)
                best_ref[g, pl.ds(i * 2 + owner, 1), :] = best

        half = GROUPS // 2
        steps = lax.shift_right_logical(total + half - 1, GROUPS.bit_length() - 1)

        @pl.loop(0, steps)
        def _(step):
            one_step(step * GROUPS, GROUPS)

        @pl.when(total > steps * GROUPS)
        def _():
            one_step(steps * GROUPS, half)

    best = jnp.concatenate([best_ref[g] for g in range(per_source)], axis=1)
    high = best.astype(jnp.bfloat16)
    rest = best - high.astype(jnp.float32)
    middle = rest.astype(jnp.bfloat16)
    low = (rest - middle.astype(jnp.float32)).astype(jnp.bfloat16)
    parts = jnp.dot(jnp.concatenate([high, middle, low], axis=0), add_ref[...], preferred_element_type=jnp.float32)
    rows = best.shape[0]
    score = (parts[:rows] + parts[rows : 2 * rows] + parts[2 * rows :]) * (1.0 / q_tok)
    if call < 2:
        out_ref[...] = score[:, :cap]
        return
    for scores, at in zip((*(ref[...] for ref in earlier), score[:, :cap]), ((0, 1, *range(4, shards, 2)), (2, 3), distances)):
        for i, d in enumerate(at):
            out_ref[pl.ds((shards - 1 - jnp.bitwise_xor(me, d)) * 2, 2), :] = scores[2 * i : 2 * i + 2]


def pair_kernel(one_ref, other_ref, out_ref):
    out_ref[0] = one_ref[...]
    out_ref[1] = other_ref[...]


def order_kernel(back_ref, out_ref):
    shards = back_ref.shape[0] // 2
    for i in range(shards):
        out_ref[0, 2 * i : 2 * i + 2] = back_ref[2 * (shards - 1 - i) : 2 * (shards - i)]


def on_device(shards, queries, passages, passage_len, slot_query, slot_passage, slot_count):
    sources, _, cap = slot_query.shape
    q_dev, q_tok, width = queries.shape
    pack = 128 // q_tok
    per_source = -(-cap // pack)
    swap = [(0, 1), (1, 0)]
    vmem, hbm, smem, anywhere = (pl.BlockSpec(memory_space=space) for space in (pltpu.VMEM, pltpu.HBM, pltpu.SMEM, pl.ANY))
    params = pltpu.CompilerParams(vmem_limit_bytes=12 * 1024 * 1024)
    row = jax.ShapeDtypeStruct((shards, 128), jnp.int32)

    def placed(space, *arrays):
        return [pltpu.with_memory_space_constraint(x, space) for x in arrays]

    def swapped(piece, d):
        return lax.ppermute(piece, "shard", [(i, i ^ d) for i in range(shards)])

    pieces = [queries, swapped(queries, 1)] + [None] * (shards - 2)
    for d in range(4, shards, 2):
        pieces[d] = swapped(queries, d)
    other_passages = lax.ppermute(passages, "sub", swap)

    calls = ((0, 1, *range(4, shards, 2)), (2, 3), range(5, shards, 2))
    sizes = tuple(map(len, calls))
    listed = [
        pltpu.SMEM(row.shape, row.dtype),
        pltpu.SMEM((len(calls),), jnp.int32),
        *(pltpu.SMEM((n * per_source + 2 * GROUPS,), jnp.int32) for n in sizes),
    ]
    theirs, own_queries, own_passages, add, *own_lists = pl.pallas_call(
        functools.partial(pack_kernel, shards, sizes, pack, per_source),
        out_shape=[
            row, *(jax.ShapeDtypeStruct(x.shape, x.dtype) for x in (queries, passages)),
            jax.ShapeDtypeStruct((per_source * 128, 128), jnp.bfloat16), *listed,
        ],
        in_specs=[hbm] * 6,
        out_specs=[vmem] * 4 + [smem] * len(listed),
        scratch_shapes=[
            pltpu.VMEM(row.shape, row.dtype),
            pltpu.VMEM((sources, cap), jnp.int32),
            pltpu.VMEM((sources, cap), jnp.int32),
            pltpu.VMEM((sources,), jnp.int32),
            pltpu.VMEM(passage_len.shape, jnp.int32),
            pltpu.SemaphoreType.DMA((5,)),
            pltpu.SemaphoreType.DMA((CHUNKS,)),
            pltpu.SemaphoreType.DMA,
        ],
        compiler_params=params,
    )(*placed(pltpu.HBM, slot_query.reshape(sources, cap), slot_passage.reshape(sources, cap), slot_count.reshape(sources), passage_len, queries, passages))
    both = pl.pallas_call(
        pair_kernel,
        out_shape=jax.ShapeDtypeStruct((2, *queries.shape), queries.dtype),
        in_specs=[vmem] * 2,
        out_specs=vmem,
        compiler_params=params,
    )(own_queries, pieces[1])
    both = swapped(both, 2)
    for d in range(5, shards, 2):
        pieces[d] = swapped(pieces[d - 1], 1)
    theirs, _ = lax.optimization_barrier((theirs, pieces[1]))
    other = lax.ppermute(theirs, "sub", swap)

    def scored(parts, lists, *earlier):
        call = len(earlier)
        n = sizes[call]
        scores = jax.ShapeDtypeStruct((2 * n if call < 2 else sources, cap), jnp.float32)
        own_rows, own_totals, *own_works = own_lists
        of_own = placed(pltpu.SMEM, own_rows, own_totals, own_works[call])
        if call:
            rows, totals, *works = lists
            of_other, others = placed(pltpu.SMEM, rows, totals, works[call]), [smem] * 3
        else:
            of_other, others = lists, [anywhere]
        return pl.pallas_call(
            functools.partial(score_kernel, shards, calls, call, pack, cap),
            out_shape=scores if call else [scores, *listed],
            in_specs=[smem] * 3 + others + [vmem] * (len(parts) + 3 + call),
            out_specs=vmem if call else [vmem] + [smem] * len(listed),
            scratch_shapes=[
                pltpu.VMEM((n, *queries.shape), queries.dtype),
                pltpu.VMEM((per_source, 2 * n, 128), jnp.float32),
                *([] if call else [pltpu.SemaphoreType.DMA]),
            ],
            compiler_params=params,
            cost_estimate=pl.CostEstimate(flops=1_000_000_000, bytes_accessed=9_000_000, transcendentals=0),
        )(*of_own, *of_other, *parts, *placed(pltpu.VMEM, own_passages, other_passages), add, *earlier)

    pieces[0] = own_queries
    near, _, far = calls
    first_scores, *lists = scored([pieces[d] for d in reversed(near)], [other])
    next_scores = scored([both], lists, first_scores)
    scores = scored([pieces[d] for d in reversed(far)], lists, first_scores, next_scores)
    order = [list(reversed(range(shards)))]
    returned = lax.all_to_all(scores, "shard", split_axis=0, concat_axis=0, axis_index_groups=order, tiled=True)
    return pl.pallas_call(
        order_kernel,
        out_shape=jax.ShapeDtypeStruct((1, sources, cap), jnp.float32),
        in_specs=[vmem],
        out_specs=vmem,
        compiler_params=params,
    )(returned)


def solution(mesh):
    return jax.shard_map(
        functools.partial(on_device, mesh.shape["shard"]),
        mesh=mesh,
        in_specs=(
            P(("groups", "shard", "sub"), None, None),
            P(("shard", "sub"), None, None),
            P(("shard", "sub")),
            P("groups", ("shard", "sub"), None),
            P("groups", ("shard", "sub"), None),
            P("groups", ("shard", "sub")),
        ),
        out_specs=P(("groups", "shard", "sub"), None, None),
        check_vma=False,
    )
```

profile of v0, /device:TPU:0, one launch (start us, length us, event | category | flops | bytes accessed | tf_op | source)
XLA Modules:
  0.0 27.1 jit_solution(3018919717643997037)
XLA Ops:
  0.0 0.5 %collective-permute-start.4 = (bf16[128,128,128]{2,1,0:T(8,128)(2,1)}, bf16[128,128,128]{2,1,0:T(8,128)(2,1)S(1)}, u32[]{:S(2)}, u32[]{:S(2)}) collective-permute-start(bf16[128,128,128]{2,1,0:T(8,128)(2,1)} %refs_5_.1), channel_id=1, source_target_pairs={{0,1},{1,0},{2,3},{3,2},{4,5},{5,4},{6,7},{7,6},{8,9},{9,8},{10,11... | collective-permute-start | bytes 12582920 | tf_op jit(solution)/shard_map/ppermute | solution.py:212
  0.5 2.5 %collective-permute-start = (bf16[8,32,128]{2,1,0:T(8,128)(2,1)}, bf16[8,32,128]{2,1,0:T(8,128)(2,1)S(1)}, u32[]{:S(2)}, u32[]{:S(2)}) collective-permute-start(bf16[8,32,128]{2,1,0:T(8,128)(2,1)} %refs_4_.1), channel_id=1, source_target_pairs={{0,2},{2,0},{4,6},{6,4},{8,10},{10,8},{12,14},{14,12},{1,3},{3,1},... | collective-permute-start | bytes 196616 | tf_op jit(solution)/shard_map/ppermute | solution.py:207
  3.0 2.6 %collective-permute-start.3 = (bf16[8,32,128]{2,1,0:T(8,128)(2,1)}, bf16[8,32,128]{2,1,0:T(8,128)(2,1)S(1)}, u32[]{:S(2)}, u32[]{:S(2)}) collective-permute-start(bf16[8,32,128]{2,1,0:T(8,128)(2,1)} %refs_4_.1), channel_id=1, source_target_pairs={{0,8},{2,10},{4,12},{6,14},{8,0},{10,2},{12,4},{14,6},{1,9},{3,11}... | collective-permute-start | bytes 196616 | tf_op jit(solution)/shard_map/ppermute | solution.py:207
  5.6 1.3 %collective-permute-start.2 = (bf16[8,32,128]{2,1,0:T(8,128)(2,1)}, bf16[8,32,128]{2,1,0:T(8,128)(2,1)S(1)}, u32[]{:S(2)}, u32[]{:S(2)}) collective-permute-start(bf16[8,32,128]{2,1,0:T(8,128)(2,1)} %refs_4_.1), channel_id=1, source_target_pairs={{0,12},{2,14},{4,8},{6,10},{8,4},{10,6},{12,0},{14,2},{1,13},{3,15... | collective-permute-start | bytes 196616 | tf_op jit(solution)/shard_map/ppermute | solution.py:207
  6.9 3.0 %shard_map.64 = (s32[8,128]{1,0:T(8,128)S(1)}, bf16[8,32,128]{2,1,0:T(8,128)(2,1)S(1)}, bf16[128,128,128]{2,1,0:T(8,128)(2,1)S(1)}, bf16[768,128]{1,0:T(8,128)(2...) custom-call(s32[16,24]{1,0:T(8,128)} %bitcast.7, ...), custom_call_target="tpu_custom_call" | custom-call | tf_op jit(solution)/shard_map/pallas_call | solution.py:221
  9.9 0.0 collective-permute-done.refs_6_.other_ref
  9.9 0.3 %collective-permute-start.7 = (bf16[2,8,32,128]{3,2,1,0:T(8,128)(2,1)S(1)}, bf16[2,8,32,128]{3,2,1,0:T(8,128)(2,1)S(1)}, u32[]{:S(2)}, u32[]{:S(2)}) collective-permute-start(bf16[2,8,32,128]{3,2,1,0:T(8,128)(2,1)S(1)} %shard_map.66), channel_id=1, source_target_pairs={{0,4},{2,6},{4,0},{6,2},{8,12},{10,14},{12,8},{14,10},{1,5},{3,7},... | collective-permute-start | bytes 393224 | tf_op jit(solution)/shard_map/ppermute | solution.py:207
  10.2 0.0 collective-permute-start.1
  10.2 0.0 collective-permute-done.3.refs_5_
  10.2 0.5 %collective-permute-start.6 = (bf16[8,32,128]{2,1,0:T(8,128)(2,1)S(1)}, bf16[8,32,128]{2,1,0:T(8,128)(2,1)S(1)}, u32[]{:S(2)}, u32[]{:S(2)}) collective-permute-start(bf16[8,32,128]{2,1,0:T(8,128)(2,1)S(1)} %collective-permute-done.3.refs_5_), channel_id=1, source_target_pairs={{0,2},{2,0},{4,6},{6,4},{8,10},{10,8},{12,14},{14,12},{1,3},{3,1},... | collective-permute-start | bytes 196616 | tf_op jit(solution)/shard_map/ppermute | solution.py:207
  10.7 1.2 %collective-permute-done.2.refs_4_ = bf16[8,32,128]{2,1,0:T(8,128)(2,1)S(1)} collective-permute-done((bf16[8,32,128]{2,1,0:T(8,128)(2,1)}, bf16[8,32,128]{2,1,0:T(8,128)(2,1)S(1)}, u32[]{:S(2)}, u32[]{:S(2)}) %collective-permute-start.2) | collective-permute-done | bytes 65568 | tf_op jit(solution)/shard_map/ppermute | solution.py:207
  11.9 0.5 %collective-permute-start.5 = (bf16[8,32,128]{2,1,0:T(8,128)(2,1)S(1)}, bf16[8,32,128]{2,1,0:T(8,128)(2,1)S(1)}, u32[]{:S(2)}, u32[]{:S(2)}) collective-permute-start(bf16[8,32,128]{2,1,0:T(8,128)(2,1)S(1)} %collective-permute-done.2.refs_4_), channel_id=1, source_target_pairs={{0,2},{2,0},{4,6},{6,4},{8,10},{10,8},{12,14},{14,12},{1,3},{3,1},... | collective-permute-start | bytes 196616 | tf_op jit(solution)/shard_map/ppermute | solution.py:207
  12.4 0.0 collective-permute-done.1.refs_3_
  12.4 0.0 collective-permute-done.4.refs_9_.refs_8_
  12.4 1.6 %shard_map.65 = (f32[8,24]{1,0:T(8,128)S(1)}, s32[8,128]{1,0:T(8,128)S(4)}, s32[3]{0:T(128)S(4)}, s32[40]{0:T(128)S(4)}, s32[28]{0:T(128)S(4)}, /*index=5*/s32[28]{0:T(128)S(4)}) custom-call(s32[8,128]{1,0:T(8,128)S(4)} %get-tuple-element.20.refs_0_, s32[3]{0:T(128)S(4)} %get-tuple-element.21.refs_1_, s32[40]{0:T(128)S(4)} %get-tuple-element.23.refs_2_, ...), custom_call_target="tpu_custom_call" | custom-call | flops 1000000000 | bytes 9000000 | tf_op jit(solution)/shard_map/pallas_call | solution.py:265
  14.0 1.0 %collective-permute-done.7.refs_6_ = bf16[2,8,32,128]{3,2,1,0:T(8,128)(2,1)S(1)} collective-permute-done((bf16[2,8,32,128]{3,2,1,0:T(8,128)(2,1)S(1)}, bf16[2,8,32,128]{3,2,1,0:T(8,128)(2,1)S(1)}, u32[]{:S(2)}, u32[]{:S(2)}) %collective-permute-start.7) | collective-permute-done | bytes 131104 | tf_op jit(solution)/shard_map/ppermute | solution.py:207
  15.0 0.9 %shard_map.67.refs_12_ = f32[4,24]{1,0:T(4,128)S(1)} custom-call(s32[8,128]{1,0:T(8,128)S(4)} %get-tuple-element.20.refs_0_, s32[3]{0:T(128)S(4)} %get-tuple-element.21.refs_1_, s32[28]{0:T(128)S(4)} %get-tuple-element.33.refs_2_, s32[8,128]{1,0:T(8,128)S(4)} %get-tuple-element.29.refs_3_, s32[3]{0:T(128)S(4)} %get-tuple-element.30.refs_4_, ...), custom_call_target="tpu_custom_call" | custom-call | flops 1000000000 | bytes 9000000 | tf_op jit(solution)/shard_map/pallas_call | solution.py:265
  16.0 0.0 collective-permute-done.6.refs_7_
  16.0 0.2 collective-permute-done.5.refs_6_
  16.2 0.8 %shard_map.68 = f32[16,24]{1,0:T(8,128)S(1)} custom-call(s32[8,128]{1,0:T(8,128)S(4)} %get-tuple-element.20.refs_0_, s32[3]{0:T(128)S(4)} %get-tuple-element.21.refs_1_, s32[28]{0:T(128)S(4)} %get-tuple-element.22.refs_2_, s32[8,128]{1,0:T(8,128)S(4)} %get-tuple-element.29.refs_3_, s32[3]{0:T(128)S(4)} %get-tuple-element.30.refs_4_, ...), custom_call_target="tpu_custom_call" | custom-call | flops 1000000000 | bytes 9000000 | tf_op jit(solution)/shard_map/pallas_call | solution.py:265
  16.9 9.6 %all_to_all.11 = f32[8,2,24]{2,1,0:T(2,128)S(1)} all-to-all(f32[8,2,24]{2,1,0:T(2,128)S(1)} %bitcast.5), channel_id=1, replica_groups={{14,12,10,8,6,4,2,0},{15,13,11,9,7,5,3,1},{30,28,26,24,22,20,18,16},{31..., dimensions={0} | all-to-all | bytes 3072 | tf_op jit(solution)/shard_map/all_to_all | solution.py:285
  26.5 0.6 %shard_map.69 = f32[1,16,24]{2,1,0:T(8,128)} custom-call(f32[16,24]{1,0:T(8,128)S(1)} %bitcast.6), custom_call_target="tpu_custom_call" | custom-call | tf_op jit(solution)/shard_map/pallas_call | solution.py:286
  (1 shorter events, 0.0 us)
Async XLA Ops:
  0.0 12.4 %collective-permute-start.4 = (bf16[128,128,128]{2,1,0:T(8,128)(2,1)}, bf16[128,128,128]{2,1,0:T(8,128)(2,1)S(1)}, u32[]{:S(2)}, u32[]{:S(2)}) collective-permute-start(bf16[128,128,128]{2,1,0:T(8,128)(2,1)} %refs_5_.1), channel_id=1, source_target_pairs={{0,1},{1,0},{2,3},{3,2},{4,5},{5,4},{6,7},{7,6},{8,9},{9,8},{10,11... | collective-permute-start | bytes 12582920 | tf_op jit(solution)/shard_map/ppermute | solution.py:212
  0.5 9.4 %collective-permute-start = (bf16[8,32,128]{2,1,0:T(8,128)(2,1)}, bf16[8,32,128]{2,1,0:T(8,128)(2,1)S(1)}, u32[]{:S(2)}, u32[]{:S(2)}) collective-permute-start(bf16[8,32,128]{2,1,0:T(8,128)(2,1)} %refs_4_.1), channel_id=1, source_target_pairs={{0,2},{2,0},{4,6},{6,4},{8,10},{10,8},{12,14},{14,12},{1,3},{3,1},... | collective-permute-start | bytes 196616 | tf_op jit(solution)/shard_map/ppermute | solution.py:207
  3.0 7.2 %collective-permute-start.3 = (bf16[8,32,128]{2,1,0:T(8,128)(2,1)}, bf16[8,32,128]{2,1,0:T(8,128)(2,1)S(1)}, u32[]{:S(2)}, u32[]{:S(2)}) collective-permute-start(bf16[8,32,128]{2,1,0:T(8,128)(2,1)} %refs_4_.1), channel_id=1, source_target_pairs={{0,8},{2,10},{4,12},{6,14},{8,0},{10,2},{12,4},{14,6},{1,9},{3,11}... | collective-permute-start | bytes 196616 | tf_op jit(solution)/shard_map/ppermute | solution.py:207
  5.6 6.3 %collective-permute-start.2 = (bf16[8,32,128]{2,1,0:T(8,128)(2,1)}, bf16[8,32,128]{2,1,0:T(8,128)(2,1)S(1)}, u32[]{:S(2)}, u32[]{:S(2)}) collective-permute-start(bf16[8,32,128]{2,1,0:T(8,128)(2,1)} %refs_4_.1), channel_id=1, source_target_pairs={{0,12},{2,14},{4,8},{6,10},{8,4},{10,6},{12,0},{14,2},{1,13},{3,15... | collective-permute-start | bytes 196616 | tf_op jit(solution)/shard_map/ppermute | solution.py:207
  9.9 5.1 %collective-permute-start.7 = (bf16[2,8,32,128]{3,2,1,0:T(8,128)(2,1)S(1)}, bf16[2,8,32,128]{3,2,1,0:T(8,128)(2,1)S(1)}, u32[]{:S(2)}, u32[]{:S(2)}) collective-permute-start(bf16[2,8,32,128]{3,2,1,0:T(8,128)(2,1)S(1)} %shard_map.66), channel_id=1, source_target_pairs={{0,4},{2,6},{4,0},{6,2},{8,12},{10,14},{12,8},{14,10},{1,5},{3,7},... | collective-permute-start | bytes 393224 | tf_op jit(solution)/shard_map/ppermute | solution.py:207
  10.2 2.2 %collective-permute-start.1 = (s32[8,128]{1,0:T(8,128)S(1)}, s32[8,128]{1,0:T(8,128)S(1)}, u32[]{:S(2)}, u32[]{:S(2)}) collective-permute-start(s32[8,128]{1,0:T(8,128)S(1)} %get-tuple-element.25), channel_id=1, source_target_pairs={{0,1},{1,0},{2,3},{3,2},{4,5},{5,4},{6,7},{7,6},{8,9},{9,8},{10,11... | collective-permute-start | bytes 12296 | tf_op jit(solution)/shard_map/ppermute | solution.py:252
  10.2 5.8 %collective-permute-start.6 = (bf16[8,32,128]{2,1,0:T(8,128)(2,1)S(1)}, bf16[8,32,128]{2,1,0:T(8,128)(2,1)S(1)}, u32[]{:S(2)}, u32[]{:S(2)}) collective-permute-start(bf16[8,32,128]{2,1,0:T(8,128)(2,1)S(1)} %collective-permute-done.3.refs_5_), channel_id=1, source_target_pairs={{0,2},{2,0},{4,6},{6,4},{8,10},{10,8},{12,14},{14,12},{1,3},{3,1},... | collective-permute-start | bytes 196616 | tf_op jit(solution)/shard_map/ppermute | solution.py:207
  11.9 4.3 %collective-permute-start.5 = (bf16[8,32,128]{2,1,0:T(8,128)(2,1)S(1)}, bf16[8,32,128]{2,1,0:T(8,128)(2,1)S(1)}, u32[]{:S(2)}, u32[]{:S(2)}) collective-permute-start(bf16[8,32,128]{2,1,0:T(8,128)(2,1)S(1)} %collective-permute-done.2.refs_4_), channel_id=1, source_target_pairs={{0,2},{2,0},{4,6},{6,4},{8,10},{10,8},{12,14},{14,12},{1,3},{3,1},... | collective-permute-start | bytes 196616 | tf_op jit(solution)/shard_map/ppermute | solution.py:207
where the time goes:
time: 27.3 us; the launch traced here: 27.1 us
  blocking collectives  9.58 us (35%)
  starting transfers between devices  8.22 us (30%)
  Pallas kernels  6.92 us (25%)
  waiting for transfers between devices  2.37 us (9%)
    all_to_all x1, blocking collectives, on_device(): lax.all_to_all(scores, 'shard', split_axis=0, concat_axis=0, axis_index_g...  9.58 us
    ppermute x6, starting transfers between devices, swapped(): return lax.ppermute(piece, 'shard', [(i, i ^ d) for i in range(shards)])  7.76 us
    pallas_call x3, Pallas kernels, scored(): pl.pallas_call(functools.partial(score_kernel, shards, calls, call, pack,...  3.35 us
    pallas_call x1, Pallas kernels, on_device(): pl.pallas_call(functools.partial(pack_kernel, shards, sizes, pack, per_so...  2.96 us
    ppermute x6, waiting for transfers between devices, swapped(): return lax.ppermute(piece, 'shard', [(i, i ^ d) for i in range(shards)])  2.36 us
    pallas_call x1, Pallas kernels, on_device(): pl.pallas_call(order_kernel, out_shape=jax.ShapeDtypeStruct((1, sources,...  0.6 us
  transfers between devices with their start and end apart: 8, of which 3 were waited for; matrix products, arithmetic and copies ran while one was open for 0% of the time, Pallas kernels for 20%

commit v1 on v0

--- a/solution.py
+++ b/solution.py
@@ -247,8 +247,8 @@
     )(own_queries, pieces[1])
     both = swapped(both, 2)
     for d in range(5, shards, 2):
-        pieces[d] = swapped(pieces[d - 1], 1)
-    theirs, _ = lax.optimization_barrier((theirs, pieces[1]))
+        pieces[d] = swapped(pieces[1], d - 1) if d == shards - 1 else swapped(pieces[d - 1], 1)
+    theirs, _ = lax.optimization_barrier((theirs, other_passages))
     other = lax.ppermute(theirs, "sub", swap)
 
     def scored(parts, lists, *earlier):

time: 27.3 us -> 27.6 us (1.011)
  starting transfers between devices: 8.22 us -> 11.1 us
  waiting for transfers between devices: 2.37 us -> 1.22 us
  blocking collectives: 9.58 us -> 8.45 us
  Pallas kernels: 6.92 us -> 6.62 us
    ppermute x6, starting transfers between devices: 7.76 us -> 10.6 us  [swapped(): return lax.ppermute(piece, 'shard', [(i, i ^ d) for i in range(shards)])]
    ppermute x6, waiting for transfers between devices: 2.36 us -> 1.21 us  [swapped(): return lax.ppermute(piece, 'shard', [(i, i ^ d) for i in range(shards)])]
    all_to_all x1, blocking collectives: 9.58 us -> 8.45 us  [on_device(): lax.all_to_all(scores, 'shard', split_axis=0, concat_axis=0, axis_index_g...]
    pallas_call x3, Pallas kernels: 3.35 us -> 3.05 us  [scored(): pl.pallas_call(functools.partial(score_kernel, shards, calls, call, pack,...]
  transfers between devices with their start and end apart: 8 -> 8, of which waited for: 3 -> 1; matrix products, arithmetic and copies ran while one was open for 0% -> 0% of each run, Pallas kernels for 20% -> 19%
where the time goes in v1:
time: 27.6 us; the launch traced here: 27.4 us
  starting transfers between devices  11.1 us (40%)
  blocking collectives  8.45 us (31%)
  Pallas kernels  6.62 us (24%)
  waiting for transfers between devices  1.22 us (4%)
    ppermute x6, starting transfers between devices, swapped(): return lax.ppermute(piece, 'shard', [(i, i ^ d) for i in range(shards)])  10.6 us
    all_to_all x1, blocking collectives, on_device(): lax.all_to_all(scores, 'shard', split_axis=0, concat_axis=0, axis_index_g...  8.45 us
    pallas_call x3, Pallas kernels, scored(): pl.pallas_call(functools.partial(score_kernel, shards, calls, call, pack,...  3.05 us
    pallas_call x1, Pallas kernels, on_device(): pl.pallas_call(functools.partial(pack_kernel, shards, sizes, pack, per_so...  2.96 us
    ppermute x6, waiting for transfers between devices, swapped(): return lax.ppermute(piece, 'shard', [(i, i ^ d) for i in range(shards)])  1.21 us
    pallas_call x1, Pallas kernels, on_device(): pl.pallas_call(order_kernel, out_shape=jax.ShapeDtypeStruct((1, sources,...  0.6 us
  transfers between devices with their start and end apart: 8, of which 1 were waited for; matrix products, arithmetic and copies ran while one was open for 0% of the time, Pallas kernels for 19%

profile of v1, /device:TPU:0, one launch (start us, length us, event | category | flops | bytes accessed | tf_op | source)
XLA Modules:
  0.0 27.4 jit_solution(5811707033866067041)
XLA Ops:
  0.0 0.5 %collective-permute-start = (bf16[128,128,128]{2,1,0:T(8,128)(2,1)}, bf16[128,128,128]{2,1,0:T(8,128)(2,1)S(1)}, u32[]{:S(2)}, u32[]{:S(2)}) collective-permute-start(bf16[128,128,128]{2,1,0:T(8,128)(2,1)} %refs_5_.1), channel_id=1, source_target_pairs={{0,1},{1,0},{2,3},{3,2},{4,5},{5,4},{6,7},{7,6},{8,9},{9,8},{10,11... | collective-permute-start | bytes 12582920 | tf_op jit(solution)/shard_map/ppermute | solution.py:212
  0.5 2.5 %collective-permute-start.4 = (bf16[8,32,128]{2,1,0:T(8,128)(2,1)}, bf16[8,32,128]{2,1,0:T(8,128)(2,1)S(1)}, u32[]{:S(2)}, u32[]{:S(2)}) collective-permute-start(bf16[8,32,128]{2,1,0:T(8,128)(2,1)} %refs_4_.1), channel_id=1, source_target_pairs={{0,2},{2,0},{4,6},{6,4},{8,10},{10,8},{12,14},{14,12},{1,3},{3,1},... | collective-permute-start | bytes 196616 | tf_op jit(solution)/shard_map/ppermute | solution.py:207
  3.0 2.6 %collective-permute-start.3 = (bf16[8,32,128]{2,1,0:T(8,128)(2,1)}, bf16[8,32,128]{2,1,0:T(8,128)(2,1)S(1)}, u32[]{:S(2)}, u32[]{:S(2)}) collective-permute-start(bf16[8,32,128]{2,1,0:T(8,128)(2,1)} %refs_4_.1), channel_id=1, source_target_pairs={{0,8},{2,10},{4,12},{6,14},{8,0},{10,2},{12,4},{14,6},{1,9},{3,11}... | collective-permute-start | bytes 196616 | tf_op jit(solution)/shard_map/ppermute | solution.py:207
  5.6 1.3 %collective-permute-start.2 = (bf16[8,32,128]{2,1,0:T(8,128)(2,1)}, bf16[8,32,128]{2,1,0:T(8,128)(2,1)S(1)}, u32[]{:S(2)}, u32[]{:S(2)}) collective-permute-start(bf16[8,32,128]{2,1,0:T(8,128)(2,1)} %refs_4_.1), channel_id=1, source_target_pairs={{0,12},{2,14},{4,8},{6,10},{8,4},{10,6},{12,0},{14,2},{1,13},{3,15... | collective-permute-start | bytes 196616 | tf_op jit(solution)/shard_map/ppermute | solution.py:207
  6.9 3.0 %shard_map.64 = (s32[8,128]{1,0:T(8,128)S(1)}, bf16[8,32,128]{2,1,0:T(8,128)(2,1)S(1)}, bf16[128,128,128]{2,1,0:T(8,128)(2,1)S(1)}, bf16[768,128]{1,0:T(8,128)(2...) custom-call(s32[16,24]{1,0:T(8,128)} %bitcast.7, ...), custom_call_target="tpu_custom_call" | custom-call | tf_op jit(solution)/shard_map/pallas_call | solution.py:221
  9.9 0.0 collective-permute-done.4.refs_6_.other_ref
  9.9 0.3 %collective-permute-start.7 = (bf16[2,8,32,128]{3,2,1,0:T(8,128)(2,1)S(1)}, bf16[2,8,32,128]{3,2,1,0:T(8,128)(2,1)S(1)}, u32[]{:S(2)}, u32[]{:S(2)}) collective-permute-start(bf16[2,8,32,128]{3,2,1,0:T(8,128)(2,1)S(1)} %shard_map.66), channel_id=1, source_target_pairs={{0,4},{2,6},{4,0},{6,2},{8,12},{10,14},{12,8},{14,10},{1,5},{3,7},... | collective-permute-start | bytes 393224 | tf_op jit(solution)/shard_map/ppermute | solution.py:207
  10.2 0.0 collective-permute-done.refs_9_.refs_8_
  10.2 0.0 collective-permute-start.1
  10.2 2.9 %collective-permute-start.5 = (bf16[8,32,128]{2,1,0:T(8,128)(2,1)S(1)}, bf16[8,32,128]{2,1,0:T(8,128)(2,1)S(1)}, u32[]{:S(2)}, u32[]{:S(2)}) collective-permute-start(bf16[8,32,128]{2,1,0:T(8,128)(2,1)S(1)} %collective-permute-done.4.refs_6_.other_ref), channel_id=1, source_target_pairs={{0,12},{2,14},{4,8},{6,10},{8,4},{10,6},{12,0},{14,2},{1,13},{3,15... | collective-permute-start | bytes 196616 | tf_op jit(solution)/shard_map/ppermute | solution.py:207
  13.1 0.0 collective-permute-done.3.refs_5_
  13.1 1.0 %collective-permute-start.6 = (bf16[8,32,128]{2,1,0:T(8,128)(2,1)S(1)}, bf16[8,32,128]{2,1,0:T(8,128)(2,1)S(1)}, u32[]{:S(2)}, u32[]{:S(2)}) collective-permute-start(bf16[8,32,128]{2,1,0:T(8,128)(2,1)S(1)} %collective-permute-done.3.refs_5_), channel_id=1, source_target_pairs={{0,2},{2,0},{4,6},{6,4},{8,10},{10,8},{12,14},{14,12},{1,3},{3,1},... | collective-permute-start | bytes 196616 | tf_op jit(solution)/shard_map/ppermute | solution.py:207
  14.1 0.0 collective-permute-done.2.refs_4_
  14.1 0.0 collective-permute-done.1.refs_3_
  14.1 1.3 %shard_map.65 = (f32[8,24]{1,0:T(8,128)S(1)}, s32[8,128]{1,0:T(8,128)S(4)}, s32[3]{0:T(128)S(4)}, s32[40]{0:T(128)S(4)}, s32[28]{0:T(128)S(4)}, /*index=5*/s32[28]{0:T(128)S(4)}) custom-call(s32[8,128]{1,0:T(8,128)S(4)} %get-tuple-element.20.refs_0_, s32[3]{0:T(128)S(4)} %get-tuple-element.21.refs_1_, s32[40]{0:T(128)S(4)} %get-tuple-element.23.refs_2_, ...), custom_call_target="tpu_custom_call" | custom-call | flops 1000000000 | bytes 9000000 | tf_op jit(solution)/shard_map/pallas_call | solution.py:265
  15.4 0.0 collective-permute-done.7.refs_6_
  15.4 0.9 %shard_map.67.refs_12_ = f32[4,24]{1,0:T(4,128)S(1)} custom-call(s32[8,128]{1,0:T(8,128)S(4)} %get-tuple-element.20.refs_0_, s32[3]{0:T(128)S(4)} %get-tuple-element.21.refs_1_, s32[28]{0:T(128)S(4)} %get-tuple-element.33.refs_2_, s32[8,128]{1,0:T(8,128)S(4)} %get-tuple-element.29.refs_3_, s32[3]{0:T(128)S(4)} %get-tuple-element.30.refs_4_, ...), custom_call_target="tpu_custom_call" | custom-call | flops 1000000000 | bytes 9000000 | tf_op jit(solution)/shard_map/pallas_call | solution.py:265
  16.4 1.2 %collective-permute-done.5.refs_6_ = bf16[8,32,128]{2,1,0:T(8,128)(2,1)S(1)} collective-permute-done((bf16[8,32,128]{2,1,0:T(8,128)(2,1)S(1)}, bf16[8,32,128]{2,1,0:T(8,128)(2,1)S(1)}, u32[]{:S(2)}, u32[]{:S(2)}) %collective-permute-start.5) | collective-permute-done | bytes 65568 | tf_op jit(solution)/shard_map/ppermute | solution.py:207
  17.6 0.0 collective-permute-done.6.refs_7_
  17.6 0.8 %shard_map.68 = f32[16,24]{1,0:T(8,128)S(1)} custom-call(s32[8,128]{1,0:T(8,128)S(4)} %get-tuple-element.20.refs_0_, s32[3]{0:T(128)S(4)} %get-tuple-element.21.refs_1_, s32[28]{0:T(128)S(4)} %get-tuple-element.22.refs_2_, s32[8,128]{1,0:T(8,128)S(4)} %get-tuple-element.29.refs_3_, s32[3]{0:T(128)S(4)} %get-tuple-element.30.refs_4_, ...), custom_call_target="tpu_custom_call" | custom-call | flops 1000000000 | bytes 9000000 | tf_op jit(solution)/shard_map/pallas_call | solution.py:265
  18.4 8.4 %all_to_all.11 = f32[8,2,24]{2,1,0:T(2,128)S(1)} all-to-all(f32[8,2,24]{2,1,0:T(2,128)S(1)} %bitcast.5), channel_id=1, replica_groups={{14,12,10,8,6,4,2,0},{15,13,11,9,7,5,3,1},{30,28,26,24,22,20,18,16},{31..., dimensions={0} | all-to-all | bytes 3072 | tf_op jit(solution)/shard_map/all_to_all | solution.py:285
  26.8 0.6 %shard_map.69 = f32[1,16,24]{2,1,0:T(8,128)} custom-call(f32[16,24]{1,0:T(8,128)S(1)} %bitcast.6), custom_call_target="tpu_custom_call" | custom-call | tf_op jit(solution)/shard_map/pallas_call | solution.py:286
  (1 shorter events, 0.0 us)
Async XLA Ops:
  0.0 10.2 %collective-permute-start = (bf16[128,128,128]{2,1,0:T(8,128)(2,1)}, bf16[128,128,128]{2,1,0:T(8,128)(2,1)S(1)}, u32[]{:S(2)}, u32[]{:S(2)}) collective-permute-start(bf16[128,128,128]{2,1,0:T(8,128)(2,1)} %refs_5_.1), channel_id=1, source_target_pairs={{0,1},{1,0},{2,3},{3,2},{4,5},{5,4},{6,7},{7,6},{8,9},{9,8},{10,11... | collective-permute-start | bytes 12582920 | tf_op jit(solution)/shard_map/ppermute | solution.py:212
  0.5 9.4 %collective-permute-start.4 = (bf16[8,32,128]{2,1,0:T(8,128)(2,1)}, bf16[8,32,128]{2,1,0:T(8,128)(2,1)S(1)}, u32[]{:S(2)}, u32[]{:S(2)}) collective-permute-start(bf16[8,32,128]{2,1,0:T(8,128)(2,1)} %refs_4_.1), channel_id=1, source_target_pairs={{0,2},{2,0},{4,6},{6,4},{8,10},{10,8},{12,14},{14,12},{1,3},{3,1},... | collective-permute-start | bytes 196616 | tf_op jit(solution)/shard_map/ppermute | solution.py:207
  3.0 10.2 %collective-permute-start.3 = (bf16[8,32,128]{2,1,0:T(8,128)(2,1)}, bf16[8,32,128]{2,1,0:T(8,128)(2,1)S(1)}, u32[]{:S(2)}, u32[]{:S(2)}) collective-permute-start(bf16[8,32,128]{2,1,0:T(8,128)(2,1)} %refs_4_.1), channel_id=1, source_target_pairs={{0,8},{2,10},{4,12},{6,14},{8,0},{10,2},{12,4},{14,6},{1,9},{3,11}... | collective-permute-start | bytes 196616 | tf_op jit(solution)/shard_map/ppermute | solution.py:207
  5.6 8.5 %collective-permute-start.2 = (bf16[8,32,128]{2,1,0:T(8,128)(2,1)}, bf16[8,32,128]{2,1,0:T(8,128)(2,1)S(1)}, u32[]{:S(2)}, u32[]{:S(2)}) collective-permute-start(bf16[8,32,128]{2,1,0:T(8,128)(2,1)} %refs_4_.1), channel_id=1, source_target_pairs={{0,12},{2,14},{4,8},{6,10},{8,4},{10,6},{12,0},{14,2},{1,13},{3,15... | collective-permute-start | bytes 196616 | tf_op jit(solution)/shard_map/ppermute | solution.py:207
  9.9 5.5 %collective-permute-start.7 = (bf16[2,8,32,128]{3,2,1,0:T(8,128)(2,1)S(1)}, bf16[2,8,32,128]{3,2,1,0:T(8,128)(2,1)S(1)}, u32[]{:S(2)}, u32[]{:S(2)}) collective-permute-start(bf16[2,8,32,128]{3,2,1,0:T(8,128)(2,1)S(1)} %shard_map.66), channel_id=1, source_target_pairs={{0,4},{2,6},{4,0},{6,2},{8,12},{10,14},{12,8},{14,10},{1,5},{3,7},... | collective-permute-start | bytes 393224 | tf_op jit(solution)/shard_map/ppermute | solution.py:207
  10.2 3.9 %collective-permute-start.1 = (s32[8,128]{1,0:T(8,128)S(1)}, s32[8,128]{1,0:T(8,128)S(1)}, u32[]{:S(2)}, u32[]{:S(2)}) collective-permute-start(s32[8,128]{1,0:T(8,128)S(1)} %get-tuple-element.25), channel_id=1, source_target_pairs={{0,1},{1,0},{2,3},{3,2},{4,5},{5,4},{6,7},{7,6},{8,9},{9,8},{10,11... | collective-permute-start | bytes 12296 | tf_op jit(solution)/shard_map/ppermute | solution.py:252
  10.2 7.4 %collective-permute-start.5 = (bf16[8,32,128]{2,1,0:T(8,128)(2,1)S(1)}, bf16[8,32,128]{2,1,0:T(8,128)(2,1)S(1)}, u32[]{:S(2)}, u32[]{:S(2)}) collective-permute-start(bf16[8,32,128]{2,1,0:T(8,128)(2,1)S(1)} %collective-permute-done.4.refs_6_.other_ref), channel_id=1, source_target_pairs={{0,12},{2,14},{4,8},{6,10},{8,4},{10,6},{12,0},{14,2},{1,13},{3,15... | collective-permute-start | bytes 196616 | tf_op jit(solution)/shard_map/ppermute | solution.py:207
  13.1 4.4 %collective-permute-start.6 = (bf16[8,32,128]{2,1,0:T(8,128)(2,1)S(1)}, bf16[8,32,128]{2,1,0:T(8,128)(2,1)S(1)}, u32[]{:S(2)}, u32[]{:S(2)}) collective-permute-start(bf16[8,32,128]{2,1,0:T(8,128)(2,1)S(1)} %collective-permute-done.3.refs_5_), channel_id=1, source_target_pairs={{0,2},{2,0},{4,6},{6,4},{8,10},{10,8},{12,14},{14,12},{1,3},{3,1},... | collective-permute-start | bytes 196616 | tf_op jit(solution)/shard_map/ppermute | solution.py:207

commit v2 on v1

--- a/solution.py
+++ b/solution.py
@@ -59,7 +59,7 @@
         pltpu.make_async_copy(own_hbm.at[pl.ds(i * size, size)], own_ref.at[pl.ds(i * size, size)], own_sems.at[i])
         for i in range(CHUNKS)
     ]
-    for copy in copies + own_copies:
+    for copy in copies + own_copies[: CHUNKS // 4]:
         copy.start()
     row = lax.broadcasted_iota(jnp.int32, add_ref.shape, 0)
     col = lax.broadcasted_iota(jnp.int32, add_ref.shape, 1)
@@ -86,6 +86,8 @@
     theirs_ref[...] = jnp.where(first, packed[:, 1], packed[:, 0])
     copy = pltpu.make_async_copy(mine_ref, row_ref, row_sem)
     copy.start()
+    for own_copy in own_copies[CHUNKS // 4 :]:
+        own_copy.start()
     copy.wait()
     list_groups(sizes, pack, per_source, row_ref, total_ref, work_refs)
     for copy in own_copies:

time: 27.6 us -> 27.7 us (level)
  Pallas kernels: 6.62 us -> 7.21 us
  waiting for transfers between devices: 1.22 us -> 0.81 us
  blocking collectives: 8.45 us -> 8.73 us
    pallas_call x3, Pallas kernels: 3.05 us -> 3.54 us  [scored(): pl.pallas_call(functools.partial(score_kernel, shards, calls, call, pack,...]
    ppermute x6, waiting for transfers between devices: 1.21 us -> 0.81 us  [swapped(): return lax.ppermute(piece, 'shard', [(i, i ^ d) for i in range(shards)])]
    all_to_all x1, blocking collectives: 8.45 us -> 8.73 us  [on_device(): lax.all_to_all(scores, 'shard', split_axis=0, concat_axis=0, axis_index_g...]
  transfers between devices with their start and end apart: 8 -> 8, of which waited for: 1 -> 1; matrix products, arithmetic and copies ran while one was open for 0% -> 0% of each run, Pallas kernels for 19% -> 21%
where the time goes in v2:
time: 27.7 us; the launch traced here: 27.8 us
  starting transfers between devices  11 us (40%)
  blocking collectives  8.73 us (32%)
  Pallas kernels  7.21 us (26%)
  waiting for transfers between devices  0.81 us (3%)
    ppermute x6, starting transfers between devices, swapped(): return lax.ppermute(piece, 'shard', [(i, i ^ d) for i in range(shards)])  10.5 us
    all_to_all x1, blocking collectives, on_device(): lax.all_to_all(scores, 'shard', split_axis=0, concat_axis=0, axis_index_g...  8.73 us
    pallas_call x3, Pallas kernels, scored(): pl.pallas_call(functools.partial(score_kernel, shards, calls, call, pack,...  3.54 us
    pallas_call x1, Pallas kernels, on_device(): pl.pallas_call(functools.partial(pack_kernel, shards, sizes, pack, per_so...  3.06 us
    ppermute x6, waiting for transfers between devices, swapped(): return lax.ppermute(piece, 'shard', [(i, i ^ d) for i in range(shards)])  0.81 us
    pallas_call x1, Pallas kernels, on_device(): pl.pallas_call(order_kernel, out_shape=jax.ShapeDtypeStruct((1, sources,...  0.6 us
  transfers between devices with their start and end apart: 8, of which 1 were waited for; matrix products, arithmetic and copies ran while one was open for 0% of the time, Pallas kernels for 21%

profile of v2, /device:TPU:0, one launch (start us, length us, event | category | flops | bytes accessed | tf_op | source)
XLA Modules:
  0.0 27.8 jit_solution(6401062257603844270)
XLA Ops:
  0.0 0.5 %collective-permute-start = (bf16[128,128,128]{2,1,0:T(8,128)(2,1)}, bf16[128,128,128]{2,1,0:T(8,128)(2,1)S(1)}, u32[]{:S(2)}, u32[]{:S(2)}) collective-permute-start(bf16[128,128,128]{2,1,0:T(8,128)(2,1)} %refs_5_.1), channel_id=1, source_target_pairs={{0,1},{1,0},{2,3},{3,2},{4,5},{5,4},{6,7},{7,6},{8,9},{9,8},{10,11... | collective-permute-start | bytes 12582920 | tf_op jit(solution)/shard_map/ppermute | solution.py:214
  0.5 2.5 %collective-permute-start.4 = (bf16[8,32,128]{2,1,0:T(8,128)(2,1)}, bf16[8,32,128]{2,1,0:T(8,128)(2,1)S(1)}, u32[]{:S(2)}, u32[]{:S(2)}) collective-permute-start(bf16[8,32,128]{2,1,0:T(8,128)(2,1)} %refs_4_.1), channel_id=1, source_target_pairs={{0,2},{2,0},{4,6},{6,4},{8,10},{10,8},{12,14},{14,12},{1,3},{3,1},... | collective-permute-start | bytes 196616 | tf_op jit(solution)/shard_map/ppermute | solution.py:209
  3.0 2.6 %collective-permute-start.3 = (bf16[8,32,128]{2,1,0:T(8,128)(2,1)}, bf16[8,32,128]{2,1,0:T(8,128)(2,1)S(1)}, u32[]{:S(2)}, u32[]{:S(2)}) collective-permute-start(bf16[8,32,128]{2,1,0:T(8,128)(2,1)} %refs_4_.1), channel_id=1, source_target_pairs={{0,8},{2,10},{4,12},{6,14},{8,0},{10,2},{12,4},{14,6},{1,9},{3,11}... | collective-permute-start | bytes 196616 | tf_op jit(solution)/shard_map/ppermute | solution.py:209
  5.6 1.3 %collective-permute-start.2 = (bf16[8,32,128]{2,1,0:T(8,128)(2,1)}, bf16[8,32,128]{2,1,0:T(8,128)(2,1)S(1)}, u32[]{:S(2)}, u32[]{:S(2)}) collective-permute-start(bf16[8,32,128]{2,1,0:T(8,128)(2,1)} %refs_4_.1), channel_id=1, source_target_pairs={{0,12},{2,14},{4,8},{6,10},{8,4},{10,6},{12,0},{14,2},{1,13},{3,15... | collective-permute-start | bytes 196616 | tf_op jit(solution)/shard_map/ppermute | solution.py:209
  6.9 3.1 %shard_map.64 = (s32[8,128]{1,0:T(8,128)S(1)}, bf16[8,32,128]{2,1,0:T(8,128)(2,1)S(1)}, bf16[128,128,128]{2,1,0:T(8,128)(2,1)S(1)}, bf16[768,128]{1,0:T(8,128)(2...) custom-call(s32[16,24]{1,0:T(8,128)} %bitcast.7, ...), custom_call_target="tpu_custom_call" | custom-call | tf_op jit(solution)/shard_map/pallas_call | solution.py:223
  10.0 0.0 collective-permute-done.4.refs_6_.other_ref
  10.0 0.3 %collective-permute-start.7 = (bf16[2,8,32,128]{3,2,1,0:T(8,128)(2,1)S(1)}, bf16[2,8,32,128]{3,2,1,0:T(8,128)(2,1)S(1)}, u32[]{:S(2)}, u32[]{:S(2)}) collective-permute-start(bf16[2,8,32,128]{3,2,1,0:T(8,128)(2,1)S(1)} %shard_map.66), channel_id=1, source_target_pairs={{0,4},{2,6},{4,0},{6,2},{8,12},{10,14},{12,8},{14,10},{1,5},{3,7},... | collective-permute-start | bytes 393224 | tf_op jit(solution)/shard_map/ppermute | solution.py:209
  10.3 0.0 collective-permute-done.refs_9_.refs_8_
  10.3 0.0 collective-permute-start.1
  10.3 2.9 %collective-permute-start.5 = (bf16[8,32,128]{2,1,0:T(8,128)(2,1)S(1)}, bf16[8,32,128]{2,1,0:T(8,128)(2,1)S(1)}, u32[]{:S(2)}, u32[]{:S(2)}) collective-permute-start(bf16[8,32,128]{2,1,0:T(8,128)(2,1)S(1)} %collective-permute-done.4.refs_6_.other_ref), channel_id=1, source_target_pairs={{0,12},{2,14},{4,8},{6,10},{8,4},{10,6},{12,0},{14,2},{1,13},{3,15... | collective-permute-start | bytes 196616 | tf_op jit(solution)/shard_map/ppermute | solution.py:209
  13.2 0.0 collective-permute-done.3.refs_5_
  13.2 0.9 %collective-permute-start.6 = (bf16[8,32,128]{2,1,0:T(8,128)(2,1)S(1)}, bf16[8,32,128]{2,1,0:T(8,128)(2,1)S(1)}, u32[]{:S(2)}, u32[]{:S(2)}) collective-permute-start(bf16[8,32,128]{2,1,0:T(8,128)(2,1)S(1)} %collective-permute-done.3.refs_5_), channel_id=1, source_target_pairs={{0,2},{2,0},{4,6},{6,4},{8,10},{10,8},{12,14},{14,12},{1,3},{3,1},... | collective-permute-start | bytes 196616 | tf_op jit(solution)/shard_map/ppermute | solution.py:209
  14.1 0.0 collective-permute-done.2.refs_4_
  14.1 0.0 collective-permute-done.1.refs_3_
  14.1 1.8 %shard_map.65 = (f32[8,24]{1,0:T(8,128)S(1)}, s32[8,128]{1,0:T(8,128)S(4)}, s32[3]{0:T(128)S(4)}, s32[40]{0:T(128)S(4)}, s32[28]{0:T(128)S(4)}, /*index=5*/s32[28]{0:T(128)S(4)}) custom-call(s32[8,128]{1,0:T(8,128)S(4)} %get-tuple-element.20.refs_0_, s32[3]{0:T(128)S(4)} %get-tuple-element.21.refs_1_, s32[40]{0:T(128)S(4)} %get-tuple-element.23.refs_2_, ...), custom_call_target="tpu_custom_call" | custom-call | flops 1000000000 | bytes 9000000 | tf_op jit(solution)/shard_map/pallas_call | solution.py:267
  15.9 0.0 collective-permute-done.7.refs_6_
  15.9 0.9 %shard_map.67.refs_12_ = f32[4,24]{1,0:T(4,128)S(1)} custom-call(s32[8,128]{1,0:T(8,128)S(4)} %get-tuple-element.20.refs_0_, s32[3]{0:T(128)S(4)} %get-tuple-element.21.refs_1_, s32[28]{0:T(128)S(4)} %get-tuple-element.33.refs_2_, s32[8,128]{1,0:T(8,128)S(4)} %get-tuple-element.29.refs_3_, s32[3]{0:T(128)S(4)} %get-tuple-element.30.refs_4_, ...), custom_call_target="tpu_custom_call" | custom-call | flops 1000000000 | bytes 9000000 | tf_op jit(solution)/shard_map/pallas_call | solution.py:267
  16.9 0.8 %collective-permute-done.5.refs_6_ = bf16[8,32,128]{2,1,0:T(8,128)(2,1)S(1)} collective-permute-done((bf16[8,32,128]{2,1,0:T(8,128)(2,1)S(1)}, bf16[8,32,128]{2,1,0:T(8,128)(2,1)S(1)}, u32[]{:S(2)}, u32[]{:S(2)}) %collective-permute-start.5) | collective-permute-done | bytes 65568 | tf_op jit(solution)/shard_map/ppermute | solution.py:209
  17.7 0.0 collective-permute-done.6.refs_7_
  17.7 0.8 %shard_map.68 = f32[16,24]{1,0:T(8,128)S(1)} custom-call(s32[8,128]{1,0:T(8,128)S(4)} %get-tuple-element.20.refs_0_, s32[3]{0:T(128)S(4)} %get-tuple-element.21.refs_1_, s32[28]{0:T(128)S(4)} %get-tuple-element.22.refs_2_, s32[8,128]{1,0:T(8,128)S(4)} %get-tuple-element.29.refs_3_, s32[3]{0:T(128)S(4)} %get-tuple-element.30.refs_4_, ...), custom_call_target="tpu_custom_call" | custom-call | flops 1000000000 | bytes 9000000 | tf_op jit(solution)/shard_map/pallas_call | solution.py:267
  18.5 8.7 %all_to_all.11 = f32[8,2,24]{2,1,0:T(2,128)S(1)} all-to-all(f32[8,2,24]{2,1,0:T(2,128)S(1)} %bitcast.5), channel_id=1, replica_groups={{14,12,10,8,6,4,2,0},{15,13,11,9,7,5,3,1},{30,28,26,24,22,20,18,16},{31..., dimensions={0} | all-to-all | bytes 3072 | tf_op jit(solution)/shard_map/all_to_all | solution.py:287
  27.2 0.6 %shard_map.69 = f32[1,16,24]{2,1,0:T(8,128)} custom-call(f32[16,24]{1,0:T(8,128)S(1)} %bitcast.6), custom_call_target="tpu_custom_call" | custom-call | tf_op jit(solution)/shard_map/pallas_call | solution.py:288
  (1 shorter events, 0.0 us)
Async XLA Ops:
  0.0 10.3 %collective-permute-start = (bf16[128,128,128]{2,1,0:T(8,128)(2,1)}, bf16[128,128,128]{2,1,0:T(8,128)(2,1)S(1)}, u32[]{:S(2)}, u32[]{:S(2)}) collective-permute-start(bf16[128,128,128]{2,1,0:T(8,128)(2,1)} %refs_5_.1), channel_id=1, source_target_pairs={{0,1},{1,0},{2,3},{3,2},{4,5},{5,4},{6,7},{7,6},{8,9},{9,8},{10,11... | collective-permute-start | bytes 12582920 | tf_op jit(solution)/shard_map/ppermute | solution.py:214
  0.5 9.5 %collective-permute-start.4 = (bf16[8,32,128]{2,1,0:T(8,128)(2,1)}, bf16[8,32,128]{2,1,0:T(8,128)(2,1)S(1)}, u32[]{:S(2)}, u32[]{:S(2)}) collective-permute-start(bf16[8,32,128]{2,1,0:T(8,128)(2,1)} %refs_4_.1), channel_id=1, source_target_pairs={{0,2},{2,0},{4,6},{6,4},{8,10},{10,8},{12,14},{14,12},{1,3},{3,1},... | collective-permute-start | bytes 196616 | tf_op jit(solution)/shard_map/ppermute | solution.py:209
  3.0 10.3 %collective-permute-start.3 = (bf16[8,32,128]{2,1,0:T(8,128)(2,1)}, bf16[8,32,128]{2,1,0:T(8,128)(2,1)S(1)}, u32[]{:S(2)}, u32[]{:S(2)}) collective-permute-start(bf16[8,32,128]{2,1,0:T(8,128)(2,1)} %refs_4_.1), channel_id=1, source_target_pairs={{0,8},{2,10},{4,12},{6,14},{8,0},{10,2},{12,4},{14,6},{1,9},{3,11}... | collective-permute-start | bytes 196616 | tf_op jit(solution)/shard_map/ppermute | solution.py:209
  5.6 8.5 %collective-permute-start.2 = (bf16[8,32,128]{2,1,0:T(8,128)(2,1)}, bf16[8,32,128]{2,1,0:T(8,128)(2,1)S(1)}, u32[]{:S(2)}, u32[]{:S(2)}) collective-permute-start(bf16[8,32,128]{2,1,0:T(8,128)(2,1)} %refs_4_.1), channel_id=1, source_target_pairs={{0,12},{2,14},{4,8},{6,10},{8,4},{10,6},{12,0},{14,2},{1,13},{3,15... | collective-permute-start | bytes 196616 | tf_op jit(solution)/shard_map/ppermute | solution.py:209
  10.0 5.9 %collective-permute-start.7 = (bf16[2,8,32,128]{3,2,1,0:T(8,128)(2,1)S(1)}, bf16[2,8,32,128]{3,2,1,0:T(8,128)(2,1)S(1)}, u32[]{:S(2)}, u32[]{:S(2)}) collective-permute-start(bf16[2,8,32,128]{3,2,1,0:T(8,128)(2,1)S(1)} %shard_map.66), channel_id=1, source_target_pairs={{0,4},{2,6},{4,0},{6,2},{8,12},{10,14},{12,8},{14,10},{1,5},{3,7},... | collective-permute-start | bytes 393224 | tf_op jit(solution)/shard_map/ppermute | solution.py:209
  10.3 3.8 %collective-permute-start.1 = (s32[8,128]{1,0:T(8,128)S(1)}, s32[8,128]{1,0:T(8,128)S(1)}, u32[]{:S(2)}, u32[]{:S(2)}) collective-permute-start(s32[8,128]{1,0:T(8,128)S(1)} %get-tuple-element.25), channel_id=1, source_target_pairs={{0,1},{1,0},{2,3},{3,2},{4,5},{5,4},{6,7},{7,6},{8,9},{9,8},{10,11... | collective-permute-start | bytes 12296 | tf_op jit(solution)/shard_map/ppermute | solution.py:254
  10.3 7.4 %collective-permute-start.5 = (bf16[8,32,128]{2,1,0:T(8,128)(2,1)S(1)}, bf16[8,32,128]{2,1,0:T(8,128)(2,1)S(1)}, u32[]{:S(2)}, u32[]{:S(2)}) collective-permute-start(bf16[8,32,128]{2,1,0:T(8,128)(2,1)S(1)} %collective-permute-done.4.refs_6_.other_ref), channel_id=1, source_target_pairs={{0,12},{2,14},{4,8},{6,10},{8,4},{10,6},{12,0},{14,2},{1,13},{3,15... | collective-permute-start | bytes 196616 | tf_op jit(solution)/shard_map/ppermute | solution.py:209
  13.2 4.4 %collective-permute-start.6 = (bf16[8,32,128]{2,1,0:T(8,128)(2,1)S(1)}, bf16[8,32,128]{2,1,0:T(8,128)(2,1)S(1)}, u32[]{:S(2)}, u32[]{:S(2)}) collective-permute-start(bf16[8,32,128]{2,1,0:T(8,128)(2,1)S(1)} %collective-permute-done.3.refs_5_), channel_id=1, source_target_pairs={{0,2},{2,0},{4,6},{6,4},{8,10},{10,8},{12,14},{14,12},{1,3},{3,1},... | collective-permute-start | bytes 196616 | tf_op jit(solution)/shard_map/ppermute | solution.py:209

commit v3 on v1

--- a/solution.py
+++ b/solution.py
@@ -38,10 +38,9 @@
         total_ref[call] = total
 
 
-def pack_kernel(shards, sizes, pack, per_source, *refs):
-    query_hbm, passage_hbm, count_hbm, length_hbm, tokens_hbm, own_hbm, theirs_ref, tokens_ref, own_ref, add_ref = refs[:10]
-    row_ref, total_ref, *work_refs = refs[10 : 12 + len(sizes)]
-    mine_ref, query_ref, passage_ref, count_ref, length_ref, sems, own_sems, row_sem = refs[12 + len(sizes) :]
+def pack_kernel(shards, *refs):
+    query_hbm, passage_hbm, count_hbm, length_hbm, tokens_hbm, own_hbm, mine_ref, theirs_ref, tokens_ref, own_ref, add_ref = refs[:11]
+    query_ref, passage_ref, count_ref, length_ref, sems, own_sems = refs[11:]
     copies = [
         pltpu.make_async_copy(src, dst, sems.at[i])
         for i, (src, dst) in enumerate(
@@ -84,10 +83,6 @@
     first = lax.axis_index("sub") == 0
     mine_ref[...] = jnp.where(first, packed[:, 0], packed[:, 1])
     theirs_ref[...] = jnp.where(first, packed[:, 1], packed[:, 0])
-    copy = pltpu.make_async_copy(mine_ref, row_ref, row_sem)
-    copy.start()
-    copy.wait()
-    list_groups(sizes, pack, per_source, row_ref, total_ref, work_refs)
     for copy in own_copies:
         copy.wait()
 
@@ -96,17 +91,17 @@
     distances = calls[call]
     n = len(distances)
     p = 1 if call == 1 else n
-    lists, refs = [refs[:3]], refs[3:]
     if call == 0:
-        other_rows, refs = refs[0], refs[1:]
-        refs, (out_ref, *other_lists, query_ref, best_ref, row_sem) = refs[: p + 3], refs[p + 3 :]
-        row_ref, total_ref, *work_refs = other_lists
-        lists.append((row_ref, total_ref, work_refs[0]))
-        copy = pltpu.make_async_copy(other_rows, row_ref, row_sem)
-        copy.start()
+        rows, refs = refs[:2], refs[2:]
+        refs, (out_ref, *outs, query_ref, best_ref, row_sems) = refs[: p + 3], refs[p + 3 :]
+        made = outs[: len(outs) // 2], outs[len(outs) // 2 :]
+        lists = [(row_ref, total_ref, work_ref) for row_ref, total_ref, work_ref, *_ in made]
+        copies = [pltpu.make_async_copy(row, each[0], row_sems.at[i]) for i, (row, each) in enumerate(zip(rows, made))]
+        for copy in copies:
+            copy.start()
     else:
-        lists.append(refs[:3])
-        refs, (out_ref, query_ref, best_ref) = refs[3:-3], refs[-3:]
+        lists = [refs[:3], refs[3:6]]
+        refs, (out_ref, query_ref, best_ref) = refs[6:-3], refs[-3:]
     pieces, passage_refs, add_ref, earlier = refs[:p], refs[p : p + 2], refs[p + 2], refs[p + 3 :]
     q_tok, width = query_ref.shape[2:]
     tok_slots = passage_refs[0].shape[1]
@@ -127,9 +122,9 @@
     for which, passages in enumerate(passage_refs):
         meta_ref, total_ref, work_ref = lists[which]
         owner = core if which == 0 else 1 - core
-        if call == 0 and which == 1:
-            copy.wait()
-            list_groups(tuple(map(len, calls)), pack, per_source, row_ref, total_ref, work_refs)
+        if call == 0:
+            copies[which].wait()
+            list_groups(tuple(map(len, calls)), pack, per_source, *made[which][:2], made[which][2:])
         total = total_ref[call]
 
         def one_step(first_group, groups):
@@ -218,23 +213,21 @@
         pltpu.SMEM((len(calls),), jnp.int32),
         *(pltpu.SMEM((n * per_source + 2 * GROUPS,), jnp.int32) for n in sizes),
     ]
-    theirs, own_queries, own_passages, add, *own_lists = pl.pallas_call(
-        functools.partial(pack_kernel, shards, sizes, pack, per_source),
+    mine, theirs, own_queries, own_passages, add = pl.pallas_call(
+        functools.partial(pack_kernel, shards),
         out_shape=[
-            row, *(jax.ShapeDtypeStruct(x.shape, x.dtype) for x in (queries, passages)),
-            jax.ShapeDtypeStruct((per_source * 128, 128), jnp.bfloat16), *listed,
+            row, row, *(jax.ShapeDtypeStruct(x.shape, x.dtype) for x in (queries, passages)),
+            jax.ShapeDtypeStruct((per_source * 128, 128), jnp.bfloat16),
         ],
         in_specs=[hbm] * 6,
-        out_specs=[vmem] * 4 + [smem] * len(listed),
+        out_specs=[vmem] * 5,
         scratch_shapes=[
-            pltpu.VMEM(row.shape, row.dtype),
             pltpu.VMEM((sources, cap), jnp.int32),
             pltpu.VMEM((sources, cap), jnp.int32),
             pltpu.VMEM((sources,), jnp.int32),
             pltpu.VMEM(passage_len.shape, jnp.int32),
             pltpu.SemaphoreType.DMA((5,)),
             pltpu.SemaphoreType.DMA((CHUNKS,)),
-            pltpu.SemaphoreType.DMA,
         ],
         compiler_params=params,
     )(*placed(pltpu.HBM, slot_query.reshape(sources, cap), slot_passage.reshape(sources, cap), slot_count.reshape(sources), passage_len, queries, passages))
@@ -255,30 +248,28 @@
         call = len(earlier)
         n = sizes[call]
         scores = jax.ShapeDtypeStruct((2 * n if call < 2 else sources, cap), jnp.float32)
-        own_rows, own_totals, *own_works = own_lists
-        of_own = placed(pltpu.SMEM, own_rows, own_totals, own_works[call])
         if call:
-            rows, totals, *works = lists
-            of_other, others = placed(pltpu.SMEM, rows, totals, works[call]), [smem] * 3
+            given = [x for rows, totals, *works in lists for x in placed(pltpu.SMEM, rows, totals, works[call])]
         else:
-            of_other, others = lists, [anywhere]
+            given = lists
         return pl.pallas_call(
             functools.partial(score_kernel, shards, calls, call, pack, cap),
-            out_shape=scores if call else [scores, *listed],
-            in_specs=[smem] * 3 + others + [vmem] * (len(parts) + 3 + call),
-            out_specs=vmem if call else [vmem] + [smem] * len(listed),
+            out_shape=scores if call else [scores, *listed, *listed],
+            in_specs=([smem] * 6 if call else [anywhere] * 2) + [vmem] * (len(parts) + 3 + call),
+            out_specs=vmem if call else [vmem] + [smem] * (2 * len(listed)),
             scratch_shapes=[
                 pltpu.VMEM((n, *queries.shape), queries.dtype),
                 pltpu.VMEM((per_source, 2 * n, 128), jnp.float32),
-                *([] if call else [pltpu.SemaphoreType.DMA]),
+                *([] if call else [pltpu.SemaphoreType.DMA((2,))]),
             ],
             compiler_params=params,
             cost_estimate=pl.CostEstimate(flops=1_000_000_000, bytes_accessed=9_000_000, transcendentals=0),
-        )(*of_own, *of_other, *parts, *placed(pltpu.VMEM, own_passages, other_passages), add, *earlier)
+        )(*given, *parts, *placed(pltpu.VMEM, own_passages, other_passages), add, *earlier)
 
     pieces[0] = own_queries
     near, _, far = calls
-    first_scores, *lists = scored([pieces[d] for d in reversed(near)], [other])
+    first_scores, *made = scored([pieces[d] for d in reversed(near)], [mine, other])
+    lists = made[: len(listed)], made[len(listed) :]
     next_scores = scored([both], lists, first_scores)
     scores = scored([pieces[d] for d in reversed(far)], lists, first_scores, next_scores)
     order = [list(reversed(range(shards)))]

time: 27.6 us -> 28.7 us (1.040)
  Pallas kernels: 6.62 us -> 8.66 us
  waiting for transfers between devices: 1.22 us -> 0.03 us
  starting transfers between devices: 11.1 us -> 11.7 us
    pallas_call x3, Pallas kernels: 3.05 us -> 5.71 us  [scored(): pl.pallas_call(functools.partial(score_kernel, shards, calls, call, pack,...]
    ppermute x6, waiting for transfers between devices: 1.21 us -> 0.02 us  [swapped(): return lax.ppermute(piece, 'shard', [(i, i ^ d) for i in range(shards)])]
    pallas_call x1, Pallas kernels: 2.96 us -> 2.33 us  [on_device(): pl.pallas_call(functools.partial(pack_kernel, shards), out_shape=[row, ro...]
    ppermute x6, starting transfers between devices: 10.6 us -> 11.3 us  [swapped(): return lax.ppermute(piece, 'shard', [(i, i ^ d) for i in range(shards)])]
  transfers between devices with their start and end apart: 8 -> 8, of which waited for: 1 -> 0; matrix products, arithmetic and copies ran while one was open for 0% -> 0% of each run, Pallas kernels for 19% -> 23%
where the time goes in v3:
time: 28.7 us; the launch traced here: 28.6 us
  starting transfers between devices  11.7 us (41%)
  Pallas kernels  8.66 us (30%)
  blocking collectives  8.18 us (29%)
    ppermute x6, starting transfers between devices, swapped(): return lax.ppermute(piece, 'shard', [(i, i ^ d) for i in range(shards)])  11.3 us
    all_to_all x1, blocking collectives, on_device(): lax.all_to_all(scores, 'shard', split_axis=0, concat_axis=0, axis_index_g...  8.18 us
    pallas_call x3, Pallas kernels, scored(): pl.pallas_call(functools.partial(score_kernel, shards, calls, call, pack,...  5.71 us
    pallas_call x1, Pallas kernels, on_device(): pl.pallas_call(functools.partial(pack_kernel, shards), out_shape=[row, ro...  2.33 us
    pallas_call x1, Pallas kernels, on_device(): pl.pallas_call(order_kernel, out_shape=jax.ShapeDtypeStruct((1, sources,...  0.6 us
  transfers between devices with their start and end apart: 8, of which 0 were waited for; matrix products, arithmetic and copies ran while one was open for 0% of the time, Pallas kernels for 23%

profile of v3, /device:TPU:0, one launch (start us, length us, event | category | flops | bytes accessed | tf_op | source)
XLA Modules:
  0.0 28.6 jit_solution(15935740812893415420)
XLA Ops:
  0.0 0.5 %collective-permute-start = (bf16[128,128,128]{2,1,0:T(8,128)(2,1)}, bf16[128,128,128]{2,1,0:T(8,128)(2,1)S(1)}, u32[]{:S(2)}, u32[]{:S(2)}) collective-permute-start(bf16[128,128,128]{2,1,0:T(8,128)(2,1)} %refs_5_.1), channel_id=1, source_target_pairs={{0,1},{1,0},{2,3},{3,2},{4,5},{5,4},{6,7},{7,6},{8,9},{9,8},{10,11... | collective-permute-start | bytes 12582920 | tf_op jit(solution)/shard_map/ppermute | solution.py:207
  0.5 2.5 %collective-permute-start.4 = (bf16[8,32,128]{2,1,0:T(8,128)(2,1)}, bf16[8,32,128]{2,1,0:T(8,128)(2,1)S(1)}, u32[]{:S(2)}, u32[]{:S(2)}) collective-permute-start(bf16[8,32,128]{2,1,0:T(8,128)(2,1)} %refs_4_.1), channel_id=1, source_target_pairs={{0,2},{2,0},{4,6},{6,4},{8,10},{10,8},{12,14},{14,12},{1,3},{3,1},... | collective-permute-start | bytes 196616 | tf_op jit(solution)/shard_map/ppermute | solution.py:202
  3.0 2.6 %collective-permute-start.3 = (bf16[8,32,128]{2,1,0:T(8,128)(2,1)}, bf16[8,32,128]{2,1,0:T(8,128)(2,1)S(1)}, u32[]{:S(2)}, u32[]{:S(2)}) collective-permute-start(bf16[8,32,128]{2,1,0:T(8,128)(2,1)} %refs_4_.1), channel_id=1, source_target_pairs={{0,8},{2,10},{4,12},{6,14},{8,0},{10,2},{12,4},{14,6},{1,9},{3,11}... | collective-permute-start | bytes 196616 | tf_op jit(solution)/shard_map/ppermute | solution.py:202
  5.6 1.3 %collective-permute-start.2 = (bf16[8,32,128]{2,1,0:T(8,128)(2,1)}, bf16[8,32,128]{2,1,0:T(8,128)(2,1)S(1)}, u32[]{:S(2)}, u32[]{:S(2)}) collective-permute-start(bf16[8,32,128]{2,1,0:T(8,128)(2,1)} %refs_4_.1), channel_id=1, source_target_pairs={{0,12},{2,14},{4,8},{6,10},{8,4},{10,6},{12,0},{14,2},{1,13},{3,15... | collective-permute-start | bytes 196616 | tf_op jit(solution)/shard_map/ppermute | solution.py:202
  6.9 2.3 %shard_map.64 = (s32[8,128]{1,0:T(8,128)S(1)}, s32[8,128]{1,0:T(8,128)S(1)}, bf16[8,32,128]{2,1,0:T(8,128)(2,1)S(1)}, bf16[128,128,128]{2,1,0:T(8,128)(2,1)S(1)}, bf16[768,128]{1,0:T(8,128)(2,1)S(1)}) custom-call(s32[16,24]{1,0:T(8,128)} %bitcast.7, s32[16,24]{1,0:T(8,128)} %bitcast.8, s32[16]{0:T(128)} %bitcast.9, s32[128]{0:T(128)} %refs_3_.1, ...), custom_call_target="tpu_custom_call" | custom-call | tf_op jit(solution)/shard_map/pallas_call | solution.py:216
  9.3 0.0 collective-permute-done.4.refs_4_.other_ref
  9.3 0.3 %collective-permute-start.7 = (bf16[2,8,32,128]{3,2,1,0:T(8,128)(2,1)S(1)}, bf16[2,8,32,128]{3,2,1,0:T(8,128)(2,1)S(1)}, u32[]{:S(2)}, u32[]{:S(2)}) collective-permute-start(bf16[2,8,32,128]{3,2,1,0:T(8,128)(2,1)S(1)} %shard_map.66), channel_id=1, source_target_pairs={{0,4},{2,6},{4,0},{6,2},{8,12},{10,14},{12,8},{14,10},{1,5},{3,7},... | collective-permute-start | bytes 393224 | tf_op jit(solution)/shard_map/ppermute | solution.py:202
  9.6 0.0 collective-permute-done.refs_7_.refs_8_.refs_9_
  9.6 0.0 collective-permute-start.1
  9.6 3.0 %collective-permute-start.5 = (bf16[8,32,128]{2,1,0:T(8,128)(2,1)S(1)}, bf16[8,32,128]{2,1,0:T(8,128)(2,1)S(1)}, u32[]{:S(2)}, u32[]{:S(2)}) collective-permute-start(bf16[8,32,128]{2,1,0:T(8,128)(2,1)S(1)} %collective-permute-done.4.refs_4_.other_ref), channel_id=1, source_target_pairs={{0,12},{2,14},{4,8},{6,10},{8,4},{10,6},{12,0},{14,2},{1,13},{3,15... | collective-permute-start | bytes 196616 | tf_op jit(solution)/shard_map/ppermute | solution.py:202
  12.6 0.0 collective-permute-done.3.refs_3_
  12.6 1.5 %collective-permute-start.6 = (bf16[8,32,128]{2,1,0:T(8,128)(2,1)S(1)}, bf16[8,32,128]{2,1,0:T(8,128)(2,1)S(1)}, u32[]{:S(2)}, u32[]{:S(2)}) collective-permute-start(bf16[8,32,128]{2,1,0:T(8,128)(2,1)S(1)} %collective-permute-done.3.refs_3_), channel_id=1, source_target_pairs={{0,2},{2,0},{4,6},{6,4},{8,10},{10,8},{12,14},{14,12},{1,3},{3,1},... | collective-permute-start | bytes 196616 | tf_op jit(solution)/shard_map/ppermute | solution.py:202
  14.1 0.0 collective-permute-done.2.refs_2_
  14.1 0.0 collective-permute-done.1.refs_1_
  14.1 3.1 %shard_map.65 = (f32[8,24]{1,0:T(8,128)S(1)}, s32[8,128]{1,0:T(8,128)S(4)}, s32[3]{0:T(128)S(4)}, s32[40]{0:T(128)S(4)}, s32[28]{0:T(128)S(4)}, /*index=5*/s32[2...) custom-call(s32[8,128]{1,0:T(8,128)S(1)} %get-tuple-element.20.refs_, ...), custom_call_target="tpu_custom_call" | custom-call | flops 1000000000 | bytes 9000000 | tf_op jit(solution)/shard_map/pallas_call | solution.py:255
  17.2 0.0 collective-permute-done.7.refs_6_
  17.2 1.3 %shard_map.67.refs_12_ = f32[4,24]{1,0:T(4,128)S(1)} custom-call(s32[8,128]{1,0:T(8,128)S(4)} %get-tuple-element.26.refs_0_, s32[3]{0:T(128)S(4)} %get-tuple-element.27.refs_1_, s32[28]{0:T(128)S(4)} %get-tuple-element.33.refs_2_, s32[8,128]{1,0:T(8,128)S(4)} %get-tuple-element.29.refs_3_, s32[3]{0:T(128)S(4)} %get-tuple-element.30.refs_4_, ...), custom_call_target="tpu_custom_call" | custom-call | flops 1000000000 | bytes 9000000 | tf_op jit(solution)/shard_map/pallas_call | solution.py:255
  18.5 0.0 collective-permute-done.5.refs_6_
  18.5 0.0 collective-permute-done.6.refs_7_
  18.5 1.4 %shard_map.68 = f32[16,24]{1,0:T(8,128)S(1)} custom-call(s32[8,128]{1,0:T(8,128)S(4)} %get-tuple-element.26.refs_0_, s32[3]{0:T(128)S(4)} %get-tuple-element.27.refs_1_, s32[28]{0:T(128)S(4)} %get-tuple-element.28.refs_2_, s32[8,128]{1,0:T(8,128)S(4)} %get-tuple-element.29.refs_3_, s32[3]{0:T(128)S(4)} %get-tuple-element.30.refs_4_, ...), custom_call_target="tpu_custom_call" | custom-call | flops 1000000000 | bytes 9000000 | tf_op jit(solution)/shard_map/pallas_call | solution.py:255
  19.9 8.2 %all_to_all.11 = f32[8,2,24]{2,1,0:T(2,128)S(1)} all-to-all(f32[8,2,24]{2,1,0:T(2,128)S(1)} %bitcast.5), channel_id=1, replica_groups={{14,12,10,8,6,4,2,0},{15,13,11,9,7,5,3,1},{30,28,26,24,22,20,18,16},{31..., dimensions={0} | all-to-all | bytes 3072 | tf_op jit(solution)/shard_map/all_to_all | solution.py:276
  28.0 0.6 %shard_map.69 = f32[1,16,24]{2,1,0:T(8,128)} custom-call(f32[16,24]{1,0:T(8,128)S(1)} %bitcast.6), custom_call_target="tpu_custom_call" | custom-call | tf_op jit(solution)/shard_map/pallas_call | solution.py:277
  (1 shorter events, 0.0 us)
Async XLA Ops:
  0.0 9.6 %collective-permute-start = (bf16[128,128,128]{2,1,0:T(8,128)(2,1)}, bf16[128,128,128]{2,1,0:T(8,128)(2,1)S(1)}, u32[]{:S(2)}, u32[]{:S(2)}) collective-permute-start(bf16[128,128,128]{2,1,0:T(8,128)(2,1)} %refs_5_.1), channel_id=1, source_target_pairs={{0,1},{1,0},{2,3},{3,2},{4,5},{5,4},{6,7},{7,6},{8,9},{9,8},{10,11... | collective-permute-start | bytes 12582920 | tf_op jit(solution)/shard_map/ppermute | solution.py:207
  0.5 8.8 %collective-permute-start.4 = (bf16[8,32,128]{2,1,0:T(8,128)(2,1)}, bf16[8,32,128]{2,1,0:T(8,128)(2,1)S(1)}, u32[]{:S(2)}, u32[]{:S(2)}) collective-permute-start(bf16[8,32,128]{2,1,0:T(8,128)(2,1)} %refs_4_.1), channel_id=1, source_target_pairs={{0,2},{2,0},{4,6},{6,4},{8,10},{10,8},{12,14},{14,12},{1,3},{3,1},... | collective-permute-start | bytes 196616 | tf_op jit(solution)/shard_map/ppermute | solution.py:202
  3.0 9.6 %collective-permute-start.3 = (bf16[8,32,128]{2,1,0:T(8,128)(2,1)}, bf16[8,32,128]{2,1,0:T(8,128)(2,1)S(1)}, u32[]{:S(2)}, u32[]{:S(2)}) collective-permute-start(bf16[8,32,128]{2,1,0:T(8,128)(2,1)} %refs_4_.1), channel_id=1, source_target_pairs={{0,8},{2,10},{4,12},{6,14},{8,0},{10,2},{12,4},{14,6},{1,9},{3,11}... | collective-permute-start | bytes 196616 | tf_op jit(solution)/shard_map/ppermute | solution.py:202
  5.6 8.5 %collective-permute-start.2 = (bf16[8,32,128]{2,1,0:T(8,128)(2,1)}, bf16[8,32,128]{2,1,0:T(8,128)(2,1)S(1)}, u32[]{:S(2)}, u32[]{:S(2)}) collective-permute-start(bf16[8,32,128]{2,1,0:T(8,128)(2,1)} %refs_4_.1), channel_id=1, source_target_pairs={{0,12},{2,14},{4,8},{6,10},{8,4},{10,6},{12,0},{14,2},{1,13},{3,15... | collective-permute-start | bytes 196616 | tf_op jit(solution)/shard_map/ppermute | solution.py:202
  9.3 7.9 %collective-permute-start.7 = (bf16[2,8,32,128]{3,2,1,0:T(8,128)(2,1)S(1)}, bf16[2,8,32,128]{3,2,1,0:T(8,128)(2,1)S(1)}, u32[]{:S(2)}, u32[]{:S(2)}) collective-permute-start(bf16[2,8,32,128]{3,2,1,0:T(8,128)(2,1)S(1)} %shard_map.66), channel_id=1, source_target_pairs={{0,4},{2,6},{4,0},{6,2},{8,12},{10,14},{12,8},{14,10},{1,5},{3,7},... | collective-permute-start | bytes 393224 | tf_op jit(solution)/shard_map/ppermute | solution.py:202
  9.6 4.5 %collective-permute-start.1 = (s32[8,128]{1,0:T(8,128)S(1)}, s32[8,128]{1,0:T(8,128)S(1)}, u32[]{:S(2)}, u32[]{:S(2)}) collective-permute-start(s32[8,128]{1,0:T(8,128)S(1)} %get-tuple-element.22), channel_id=1, source_target_pairs={{0,1},{1,0},{2,3},{3,2},{4,5},{5,4},{6,7},{7,6},{8,9},{9,8},{10,11... | collective-permute-start | bytes 12296 | tf_op jit(solution)/shard_map/ppermute | solution.py:245
  9.6 8.9 %collective-permute-start.5 = (bf16[8,32,128]{2,1,0:T(8,128)(2,1)S(1)}, bf16[8,32,128]{2,1,0:T(8,128)(2,1)S(1)}, u32[]{:S(2)}, u32[]{:S(2)}) collective-permute-start(bf16[8,32,128]{2,1,0:T(8,128)(2,1)S(1)} %collective-permute-done.4.refs_4_.other_ref), channel_id=1, source_target_pairs={{0,12},{2,14},{4,8},{6,10},{8,4},{10,6},{12,0},{14,2},{1,13},{3,15... | collective-permute-start | bytes 196616 | tf_op jit(solution)/shard_map/ppermute | solution.py:202
  12.6 5.9 %collective-permute-start.6 = (bf16[8,32,128]{2,1,0:T(8,128)(2,1)S(1)}, bf16[8,32,128]{2,1,0:T(8,128)(2,1)S(1)}, u32[]{:S(2)}, u32[]{:S(2)}) collective-permute-start(bf16[8,32,128]{2,1,0:T(8,128)(2,1)S(1)} %collective-permute-done.3.refs_3_), channel_id=1, source_target_pairs={{0,2},{2,0},{4,6},{6,4},{8,10},{10,8},{12,14},{14,12},{1,3},{3,1},... | collective-permute-start | bytes 196616 | tf_op jit(solution)/shard_map/ppermute | solution.py:202

commit v4 on v3

--- a/solution.py
+++ b/solution.py
@@ -33,7 +33,7 @@
                 total = list_source(i, total)
         else:
             total = lax.fori_loop(0, n, list_source, 0)
-        for g in range(GROUPS):
+        for g in range(GROUPS // 2 - 1):
             work_ref[total + g] = 0
         total_ref[call] = total
 

time: 28.7 us -> 27.4 us (0.955)
  Pallas kernels: 8.66 us -> 6.53 us
  blocking collectives: 8.18 us -> 8.89 us
    pallas_call x3, Pallas kernels: 5.71 us -> 3.59 us  [scored(): pl.pallas_call(functools.partial(score_kernel, shards, calls, call, pack,...]
    all_to_all x1, blocking collectives: 8.18 us -> 8.89 us  [on_device(): lax.all_to_all(scores, 'shard', split_axis=0, concat_axis=0, axis_index_g...]
  transfers between devices with their start and end apart: 8 -> 8, of which waited for: 0 -> 0; matrix products, arithmetic and copies ran while one was open for 0% -> 0% of each run, Pallas kernels for 23% -> 19%
where the time goes in v4:
time: 27.4 us; the launch traced here: 27.2 us
  starting transfers between devices  11.7 us (43%)
  blocking collectives  8.89 us (32%)
  Pallas kernels  6.53 us (24%)
    ppermute x6, starting transfers between devices, swapped(): return lax.ppermute(piece, 'shard', [(i, i ^ d) for i in range(shards)])  11.3 us
    all_to_all x1, blocking collectives, on_device(): lax.all_to_all(scores, 'shard', split_axis=0, concat_axis=0, axis_index_g...  8.89 us
    pallas_call x3, Pallas kernels, scored(): pl.pallas_call(functools.partial(score_kernel, shards, calls, call, pack,...  3.59 us
    pallas_call x1, Pallas kernels, on_device(): pl.pallas_call(functools.partial(pack_kernel, shards), out_shape=[row, ro...  2.33 us
    pallas_call x1, Pallas kernels, on_device(): pl.pallas_call(order_kernel, out_shape=jax.ShapeDtypeStruct((1, sources,...  0.6 us
  transfers between devices with their start and end apart: 8, of which 0 were waited for; matrix products, arithmetic and copies ran while one was open for 0% of the time, Pallas kernels for 19%

profile of v4, /device:TPU:0, one launch (start us, length us, event | category | flops | bytes accessed | tf_op | source)
XLA Modules:
  0.0 27.2 jit_solution(15754925433841244441)
XLA Ops:
  0.0 0.5 %collective-permute-start = (bf16[128,128,128]{2,1,0:T(8,128)(2,1)}, bf16[128,128,128]{2,1,0:T(8,128)(2,1)S(1)}, u32[]{:S(2)}, u32[]{:S(2)}) collective-permute-start(bf16[128,128,128]{2,1,0:T(8,128)(2,1)} %refs_5_.1), channel_id=1, source_target_pairs={{0,1},{1,0},{2,3},{3,2},{4,5},{5,4},{6,7},{7,6},{8,9},{9,8},{10,11... | collective-permute-start | bytes 12582920 | tf_op jit(solution)/shard_map/ppermute | solution.py:207
  0.5 2.5 %collective-permute-start.4 = (bf16[8,32,128]{2,1,0:T(8,128)(2,1)}, bf16[8,32,128]{2,1,0:T(8,128)(2,1)S(1)}, u32[]{:S(2)}, u32[]{:S(2)}) collective-permute-start(bf16[8,32,128]{2,1,0:T(8,128)(2,1)} %refs_4_.1), channel_id=1, source_target_pairs={{0,2},{2,0},{4,6},{6,4},{8,10},{10,8},{12,14},{14,12},{1,3},{3,1},... | collective-permute-start | bytes 196616 | tf_op jit(solution)/shard_map/ppermute | solution.py:202
  3.0 2.6 %collective-permute-start.3 = (bf16[8,32,128]{2,1,0:T(8,128)(2,1)}, bf16[8,32,128]{2,1,0:T(8,128)(2,1)S(1)}, u32[]{:S(2)}, u32[]{:S(2)}) collective-permute-start(bf16[8,32,128]{2,1,0:T(8,128)(2,1)} %refs_4_.1), channel_id=1, source_target_pairs={{0,8},{2,10},{4,12},{6,14},{8,0},{10,2},{12,4},{14,6},{1,9},{3,11}... | collective-permute-start | bytes 196616 | tf_op jit(solution)/shard_map/ppermute | solution.py:202
  5.6 1.3 %collective-permute-start.2 = (bf16[8,32,128]{2,1,0:T(8,128)(2,1)}, bf16[8,32,128]{2,1,0:T(8,128)(2,1)S(1)}, u32[]{:S(2)}, u32[]{:S(2)}) collective-permute-start(bf16[8,32,128]{2,1,0:T(8,128)(2,1)} %refs_4_.1), channel_id=1, source_target_pairs={{0,12},{2,14},{4,8},{6,10},{8,4},{10,6},{12,0},{14,2},{1,13},{3,15... | collective-permute-start | bytes 196616 | tf_op jit(solution)/shard_map/ppermute | solution.py:202
  6.9 2.3 %shard_map.64 = (s32[8,128]{1,0:T(8,128)S(1)}, s32[8,128]{1,0:T(8,128)S(1)}, bf16[8,32,128]{2,1,0:T(8,128)(2,1)S(1)}, bf16[128,128,128]{2,1,0:T(8,128)(2,1)S(1)}, bf16[768,128]{1,0:T(8,128)(2,1)S(1)}) custom-call(s32[16,24]{1,0:T(8,128)} %bitcast.7, s32[16,24]{1,0:T(8,128)} %bitcast.8, s32[16]{0:T(128)} %bitcast.9, s32[128]{0:T(128)} %refs_3_.1, ...), custom_call_target="tpu_custom_call" | custom-call | tf_op jit(solution)/shard_map/pallas_call | solution.py:216
  9.3 0.0 collective-permute-done.4.refs_4_.other_ref
  9.3 0.3 %collective-permute-start.7 = (bf16[2,8,32,128]{3,2,1,0:T(8,128)(2,1)S(1)}, bf16[2,8,32,128]{3,2,1,0:T(8,128)(2,1)S(1)}, u32[]{:S(2)}, u32[]{:S(2)}) collective-permute-start(bf16[2,8,32,128]{3,2,1,0:T(8,128)(2,1)S(1)} %shard_map.66), channel_id=1, source_target_pairs={{0,4},{2,6},{4,0},{6,2},{8,12},{10,14},{12,8},{14,10},{1,5},{3,7},... | collective-permute-start | bytes 393224 | tf_op jit(solution)/shard_map/ppermute | solution.py:202
  9.6 0.0 collective-permute-done.refs_7_.refs_8_.refs_9_
  9.6 0.0 collective-permute-start.1
  9.6 3.0 %collective-permute-start.5 = (bf16[8,32,128]{2,1,0:T(8,128)(2,1)S(1)}, bf16[8,32,128]{2,1,0:T(8,128)(2,1)S(1)}, u32[]{:S(2)}, u32[]{:S(2)}) collective-permute-start(bf16[8,32,128]{2,1,0:T(8,128)(2,1)S(1)} %collective-permute-done.4.refs_4_.other_ref), channel_id=1, source_target_pairs={{0,12},{2,14},{4,8},{6,10},{8,4},{10,6},{12,0},{14,2},{1,13},{3,15... | collective-permute-start | bytes 196616 | tf_op jit(solution)/shard_map/ppermute | solution.py:202
  12.6 0.0 collective-permute-done.3.refs_3_
  12.6 1.5 %collective-permute-start.6 = (bf16[8,32,128]{2,1,0:T(8,128)(2,1)S(1)}, bf16[8,32,128]{2,1,0:T(8,128)(2,1)S(1)}, u32[]{:S(2)}, u32[]{:S(2)}) collective-permute-start(bf16[8,32,128]{2,1,0:T(8,128)(2,1)S(1)} %collective-permute-done.3.refs_3_), channel_id=1, source_target_pairs={{0,2},{2,0},{4,6},{6,4},{8,10},{10,8},{12,14},{14,12},{1,3},{3,1},... | collective-permute-start | bytes 196616 | tf_op jit(solution)/shard_map/ppermute | solution.py:202
  14.1 0.0 collective-permute-done.2.refs_2_
  14.1 0.0 collective-permute-done.1.refs_1_
  14.1 1.8 %shard_map.65 = (f32[8,24]{1,0:T(8,128)S(1)}, s32[8,128]{1,0:T(8,128)S(4)}, s32[3]{0:T(128)S(4)}, s32[40]{0:T(128)S(4)}, s32[28]{0:T(128)S(4)}, /*index=5*/s32[2...) custom-call(s32[8,128]{1,0:T(8,128)S(1)} %get-tuple-element.20.refs_, ...), custom_call_target="tpu_custom_call" | custom-call | flops 1000000000 | bytes 9000000 | tf_op jit(solution)/shard_map/pallas_call | solution.py:255
  16.0 0.0 collective-permute-done.7.refs_6_
  16.0 0.9 %shard_map.67.refs_12_ = f32[4,24]{1,0:T(4,128)S(1)} custom-call(s32[8,128]{1,0:T(8,128)S(4)} %get-tuple-element.26.refs_0_, s32[3]{0:T(128)S(4)} %get-tuple-element.27.refs_1_, s32[28]{0:T(128)S(4)} %get-tuple-element.33.refs_2_, s32[8,128]{1,0:T(8,128)S(4)} %get-tuple-element.29.refs_3_, s32[3]{0:T(128)S(4)} %get-tuple-element.30.refs_4_, ...), custom_call_target="tpu_custom_call" | custom-call | flops 1000000000 | bytes 9000000 | tf_op jit(solution)/shard_map/pallas_call | solution.py:255
  16.9 0.0 collective-permute-done.5.refs_6_
  16.9 0.0 collective-permute-done.6.refs_7_
  16.9 0.8 %shard_map.68 = f32[16,24]{1,0:T(8,128)S(1)} custom-call(s32[8,128]{1,0:T(8,128)S(4)} %get-tuple-element.26.refs_0_, s32[3]{0:T(128)S(4)} %get-tuple-element.27.refs_1_, s32[28]{0:T(128)S(4)} %get-tuple-element.28.refs_2_, s32[8,128]{1,0:T(8,128)S(4)} %get-tuple-element.29.refs_3_, s32[3]{0:T(128)S(4)} %get-tuple-element.30.refs_4_, ...), custom_call_target="tpu_custom_call" | custom-call | flops 1000000000 | bytes 9000000 | tf_op jit(solution)/shard_map/pallas_call | solution.py:255
  17.8 8.9 %all_to_all.11 = f32[8,2,24]{2,1,0:T(2,128)S(1)} all-to-all(f32[8,2,24]{2,1,0:T(2,128)S(1)} %bitcast.5), channel_id=1, replica_groups={{14,12,10,8,6,4,2,0},{15,13,11,9,7,5,3,1},{30,28,26,24,22,20,18,16},{31..., dimensions={0} | all-to-all | bytes 3072 | tf_op jit(solution)/shard_map/all_to_all | solution.py:276
  26.6 0.6 %shard_map.69 = f32[1,16,24]{2,1,0:T(8,128)} custom-call(f32[16,24]{1,0:T(8,128)S(1)} %bitcast.6), custom_call_target="tpu_custom_call" | custom-call | tf_op jit(solution)/shard_map/pallas_call | solution.py:277
  (1 shorter events, 0.0 us)
Async XLA Ops:
  0.0 9.6 %collective-permute-start = (bf16[128,128,128]{2,1,0:T(8,128)(2,1)}, bf16[128,128,128]{2,1,0:T(8,128)(2,1)S(1)}, u32[]{:S(2)}, u32[]{:S(2)}) collective-permute-start(bf16[128,128,128]{2,1,0:T(8,128)(2,1)} %refs_5_.1), channel_id=1, source_target_pairs={{0,1},{1,0},{2,3},{3,2},{4,5},{5,4},{6,7},{7,6},{8,9},{9,8},{10,11... | collective-permute-start | bytes 12582920 | tf_op jit(solution)/shard_map/ppermute | solution.py:207
  0.5 8.8 %collective-permute-start.4 = (bf16[8,32,128]{2,1,0:T(8,128)(2,1)}, bf16[8,32,128]{2,1,0:T(8,128)(2,1)S(1)}, u32[]{:S(2)}, u32[]{:S(2)}) collective-permute-start(bf16[8,32,128]{2,1,0:T(8,128)(2,1)} %refs_4_.1), channel_id=1, source_target_pairs={{0,2},{2,0},{4,6},{6,4},{8,10},{10,8},{12,14},{14,12},{1,3},{3,1},... | collective-permute-start | bytes 196616 | tf_op jit(solution)/shard_map/ppermute | solution.py:202
  3.0 9.6 %collective-permute-start.3 = (bf16[8,32,128]{2,1,0:T(8,128)(2,1)}, bf16[8,32,128]{2,1,0:T(8,128)(2,1)S(1)}, u32[]{:S(2)}, u32[]{:S(2)}) collective-permute-start(bf16[8,32,128]{2,1,0:T(8,128)(2,1)} %refs_4_.1), channel_id=1, source_target_pairs={{0,8},{2,10},{4,12},{6,14},{8,0},{10,2},{12,4},{14,6},{1,9},{3,11}... | collective-permute-start | bytes 196616 | tf_op jit(solution)/shard_map/ppermute | solution.py:202
  5.6 8.5 %collective-permute-start.2 = (bf16[8,32,128]{2,1,0:T(8,128)(2,1)}, bf16[8,32,128]{2,1,0:T(8,128)(2,1)S(1)}, u32[]{:S(2)}, u32[]{:S(2)}) collective-permute-start(bf16[8,32,128]{2,1,0:T(8,128)(2,1)} %refs_4_.1), channel_id=1, source_target_pairs={{0,12},{2,14},{4,8},{6,10},{8,4},{10,6},{12,0},{14,2},{1,13},{3,15... | collective-permute-start | bytes 196616 | tf_op jit(solution)/shard_map/ppermute | solution.py:202
  9.3 6.7 %collective-permute-start.7 = (bf16[2,8,32,128]{3,2,1,0:T(8,128)(2,1)S(1)}, bf16[2,8,32,128]{3,2,1,0:T(8,128)(2,1)S(1)}, u32[]{:S(2)}, u32[]{:S(2)}) collective-permute-start(bf16[2,8,32,128]{3,2,1,0:T(8,128)(2,1)S(1)} %shard_map.66), channel_id=1, source_target_pairs={{0,4},{2,6},{4,0},{6,2},{8,12},{10,14},{12,8},{14,10},{1,5},{3,7},... | collective-permute-start | bytes 393224 | tf_op jit(solution)/shard_map/ppermute | solution.py:202
  9.6 4.5 %collective-permute-start.1 = (s32[8,128]{1,0:T(8,128)S(1)}, s32[8,128]{1,0:T(8,128)S(1)}, u32[]{:S(2)}, u32[]{:S(2)}) collective-permute-start(s32[8,128]{1,0:T(8,128)S(1)} %get-tuple-element.22), channel_id=1, source_target_pairs={{0,1},{1,0},{2,3},{3,2},{4,5},{5,4},{6,7},{7,6},{8,9},{9,8},{10,11... | collective-permute-start | bytes 12296 | tf_op jit(solution)/shard_map/ppermute | solution.py:245
  9.6 7.4 %collective-permute-start.5 = (bf16[8,32,128]{2,1,0:T(8,128)(2,1)S(1)}, bf16[8,32,128]{2,1,0:T(8,128)(2,1)S(1)}, u32[]{:S(2)}, u32[]{:S(2)}) collective-permute-start(bf16[8,32,128]{2,1,0:T(8,128)(2,1)S(1)} %collective-permute-done.4.refs_4_.other_ref), channel_id=1, source_target_pairs={{0,12},{2,14},{4,8},{6,10},{8,4},{10,6},{12,0},{14,2},{1,13},{3,15... | collective-permute-start | bytes 196616 | tf_op jit(solution)/shard_map/ppermute | solution.py:202
  12.6 4.4 %collective-permute-start.6 = (bf16[8,32,128]{2,1,0:T(8,128)(2,1)S(1)}, bf16[8,32,128]{2,1,0:T(8,128)(2,1)S(1)}, u32[]{:S(2)}, u32[]{:S(2)}) collective-permute-start(bf16[8,32,128]{2,1,0:T(8,128)(2,1)S(1)} %collective-permute-done.3.refs_3_), channel_id=1, source_target_pairs={{0,2},{2,0},{4,6},{6,4},{8,10},{10,8},{12,14},{14,12},{1,3},{3,1},... | collective-permute-start | bytes 196616 | tf_op jit(solution)/shard_map/ppermute | solution.py:202
